TPU v7x, 128 devices: a whole 4x4x4 slice. The times are simulated.
128 devices in a mesh: gx: 8 (over x, core), gz: 16 (over y, z).
Axes of the slice: x: 4, y: 4, z: 4, core: 2. Of those that a mesh axis runs over, the one named last changes fastest.
Arguments:
- velocity: float32 [3, 256, 512, 256], P(None, 'gz', 'gx'), may hold values from -6 to 6
- mean_flow: float32 [256], replicated, may hold values from 0.2 to 1
- fibres: float32 [6, 524288], P(None, ('gx', 'gz')), may hold values from -0.6 to 0.6
- moves: int32 [524288, 1], P(('gx', 'gz')), may hold values from 0 to 8, as said below
- grad_rows: int32 [24576], P(('gx', 'gz')), may hold values from 0 to 2047
- grad_readers: int32 [24576, 1], P(('gx', 'gz')), may hold values from 0 to 127; in each aligned block of 192 rows (0 to 191, 192 to 383, ...) at most 2 rows name the same one
- fibre_cell: int32 [655360], P(('gx', 'gz')), may hold values from 0 to 32767
Outputs:
- advanced_flow: float32 [3, 256, 512, 256], P(None, 'gz', 'gx')
- fibres_out: float32 [6, 655360], P(None, ('gx', 'gz'))
Inputs may be any that keep to these rules, and one draw needn't show every extreme that they name: `moves`: of one device's fibres at most 128 take any one code other than 4, and on every device some code other than 4 is taken by exactly 128; all other fibres have code 4. `grad_readers`: of one device's list entries at most 2 name the same reader, a bound that some block reaches.
All inputs are finite; a program needn't handle non-finite values.
Results may differ from a plain program's by a relative error of at most 0.0003.
Values sent between devices are 32-bit elements; how exact they have to be, the bound alone decides.
A program may use at most 128 MiB of HBM per device.

v0:
```python
import jax
import jax.numpy as jnp
from jax import lax
from jax.sharding import PartitionSpec as P

SUB = 2
FIB_DEV = 4096
CAP = 128
SLOT_DEV = 5120
RCAP = 2


DIFFUSION = 0.1
ADVECTION = 0.4
SHAPE_FACTOR = 0.9
TURN_STEP = 0.25


def extended(cells, sides, width):
    for axis, dim in sides:
        count = lax.axis_size(axis)
        head = lax.slice_in_dim(cells, 0, width, axis=dim)
        tail = lax.slice_in_dim(cells, cells.shape[dim] - width, cells.shape[dim], axis=dim)
        cells = jnp.concatenate(
            [
                lax.ppermute(tail, axis, [(i, (i + 1) % count) for i in range(count)]),
                cells,
                lax.ppermute(head, axis, [((i + 1) % count, i) for i in range(count)]),
            ],
            axis=dim,
        )
    return cells


def from_behind(block, axis, distance):
    devices = range(lax.axis_size(axis))
    route = [((i - distance) % len(devices), i) for i in devices]
    return lax.ppermute(block, axis, route)


def update(padded, mean_flow):
    centre = padded[:, 1:-1, 1:-1, 1:-1]
    beside_all = padded[:, 2:, 1:-1, 1:-1] + padded[:, :-2, 1:-1, 1:-1]
    beside_all = beside_all + padded[:, 1:-1, 2:, 1:-1] + padded[:, 1:-1, :-2, 1:-1]
    beside_all = beside_all + padded[:, 1:-1, 1:-1, 2:] + padded[:, 1:-1, 1:-1, :-2]
    streamwise = 0.5 * (padded[:, 1:-1, 2:, 1:-1] - padded[:, 1:-1, :-2, 1:-1])
    return centre + DIFFUSION * (beside_all - 6.0 * centre) - ADVECTION * mean_flow * streamwise


def gradient(padded):
    along_x = 0.5 * (padded[:, 1:-1, 2:, 1:-1] - padded[:, 1:-1, :-2, 1:-1])
    along_y = 0.5 * (padded[:, 1:-1, 1:-1, 2:] - padded[:, 1:-1, 1:-1, :-2])
    along_z = 0.5 * (padded[:, 2:, 1:-1, 1:-1] - padded[:, :-2, 1:-1, 1:-1])
    return jnp.stack([along_x, along_y, along_z], axis=1)


def extend(flow_field):
    padded = extended(flow_field, (("gz", 1), ("gx", 2)), 1)
    return jnp.pad(padded, ((0, 0), (0, 0), (0, 0), (1, 1)))


def pack_rows(row_table, wanted, readers, devices):
    onehot = (readers[:, None] == jnp.arange(devices, dtype=jnp.int32)[None, :]).astype(jnp.int32)
    slot_rank = jnp.sum((jnp.cumsum(onehot, axis=0) - onehot) * onehot, axis=1)
    slot_pos = readers * RCAP + slot_rank
    picked = jnp.take(row_table, wanted, axis=1)
    empty = jnp.zeros((row_table.shape[0], devices * RCAP, row_table.shape[2]), jnp.float32)
    return empty.at[:, slot_pos].set(picked)


def code_offset(code):
    return code * CAP if code <= 4 else FIB_DEV + (code - 1) * CAP


def code_width(code):
    return FIB_DEV if code == 4 else CAP


def pack_fibres(records, move_code):
    onehot = (move_code[:, None] == jnp.arange(9, dtype=jnp.int32)[None, :]).astype(jnp.int32)
    slot_rank = jnp.sum((jnp.cumsum(onehot, axis=0) - onehot) * onehot, axis=1)
    offset = jnp.where(move_code <= 4, move_code * CAP, FIB_DEV + (move_code - 1) * CAP)
    slot_pos = offset + slot_rank
    return jnp.zeros((records.shape[0], SLOT_DEV), jnp.float32).at[:, slot_pos].set(records)


def jeffery(records, tensor):
    orient = records[3:6]
    along = jnp.stack(
        [
            tensor[3 * comp] * orient[0]
            + tensor[3 * comp + 1] * orient[1]
            + tensor[3 * comp + 2] * orient[2]
            for comp in range(3)
        ]
    )
    across = jnp.stack(
        [
            tensor[comp] * orient[0] + tensor[3 + comp] * orient[1] + tensor[6 + comp] * orient[2]
            for comp in range(3)
        ]
    )
    strain = 0.5 * (along + across)
    rotation = 0.5 * (along - across)
    stretch = orient[0] * along[0] + orient[1] * along[1] + orient[2] * along[2]
    turned = orient + TURN_STEP * (rotation + SHAPE_FACTOR * (strain - stretch * orient))
    return jnp.concatenate([records[0:3], turned], axis=0)


def code_piece(records, code):
    start = code_offset(code)
    return records[:, start : start + code_width(code)]


def per_device(velocity, mean_flow, fibres, moves, grad_rows, grad_readers, fibre_cell):
    count_x = lax.axis_size("gx")
    count_z = lax.axis_size("gz")
    devices = count_x * count_z
    flow_field = velocity
    for substep in range(SUB):
        flow_field = update(extend(flow_field), mean_flow)
    grads = gradient(extend(flow_field))
    row_count = grads.shape[2] * grads.shape[3] * grads.shape[4] // 128
    row_table = grads.reshape(9, row_count, 128)
    send_rows = pack_rows(row_table, grad_rows, grad_readers[:, 0], devices)
    received = lax.all_to_all(send_rows, ("gx", "gz"), split_axis=1, concat_axis=1, tiled=True)
    flat_table = received.reshape(9, devices * RCAP * 128)
    sending = pack_fibres(fibres, moves[:, 0])
    parts_list = []
    for move_code in range(9):
        block_part = code_piece(sending, move_code)
        step_x = move_code // 3 - 1
        step_z = move_code % 3 - 1
        if step_x != 0:
            block_part = from_behind(block_part, "gx", step_x)
        if step_z != 0:
            block_part = from_behind(block_part, "gz", step_z)
        parts_list.append(block_part)
    arrived = jnp.concatenate(parts_list, axis=1)
    tensor = jnp.take(flat_table, fibre_cell, axis=1)
    return (flow_field, jeffery(arrived, tensor))


def solution(mesh):
    return jax.shard_map(
        per_device,
        mesh=mesh,
        in_specs=(
            P(None, "gz", "gx", None),
            P(),
            P(None, ("gx", "gz")),
            P(("gx", "gz"), None),
            P(("gx", "gz")),
            P(("gx", "gz"), None),
            P(("gx", "gz")),
        ),
        out_specs=(P(None, "gz", "gx", None), P(None, ("gx", "gz"))),
        check_vma=False,
    )
```

profile of v0, /device:TPU:0, one launch (start us, length us, event | category | flops | bytes accessed | tf_op | source)
XLA Modules:
  0.0 252.5 jit_solution(8993672552780653096)
XLA Ops:
  4.5 4.6 %collective-permute-start = (f32[3,1,64,256]{3,2,1,0:T(8,128)}, f32[3,1,64,256]{3,2,1,0:T(8,128)S(1)}, u32[]{:S(2)}, u32[]{:S(2)}) collective-permute-start(f32[3,1,64,256]{3,2,1,0:T(8,128)} %get-tuple-element.22), channel_id=1, source_target_pairs={{1,0},{2,1},{3,2},{4,3},{5,4},{6,5},{7,6},{8,7},{9,8},{10,9},{11,1... | collective-permute-start | bytes 589832 | tf_op jit(solution)/shard_map/ppermute | solution.py:28
  17.7 12.7 %scatter_custom_fusion = f32[6,5120]{0,1:T(8,128)} fusion(s32[4096]{0:T(1024)S(1)} %bitcast.53, f32[4096,6]{1,0:T(8,128)} %copy.125, f32[]{:T(128)} %constant.24.clone.1), kind=kCustom, calls=%fused_computation.65 | custom fusion | bytes 123392 | tf_op jit(solution)/shard_map/scatter | solution.py:84
  48.2 3.0 %collective-permute-done.3 = f32[3,18,1,256]{3,2,1,0:T(1,128)S(1)} collective-permute-done((f32[3,18,1,256]{3,2,1,0:T(1,128)S(1)}, f32[3,18,1,256]{3,2,1,0:T(1,128)S(1)}, u32[]{:S(2)}, u32[]{:S(2)}) %collective-permute-start.3) | collective-permute-done | bytes 55328 | tf_op jit(solution)/shard_map/ppermute | solution.py:26
  54.2 4.6 %fusion.19 = f32[3,16,64,256]{3,2,1,0:T(8,128)S(1)} fusion(f32[3,16,64,256]{3,2,1,0:T(8,128)S(1)} %copy-done.1, f32[3,18,66,258]{3,2,1,0:T(8,128)S(1)} %select_maximum_fusion.8, f32[3,1,64,256]{3,2,1,0:T(8,128)S(1)} %collective-permute-done.1, f32[3,1,64,256]{3,2,1,0:T(8,128)S(1)} %collective-permute-done, f32[3,18,1,256]{3,2,1,0:T(1,128)S(1)} %collective-permute-done.2, ...), kind=kLoop, calls=%fused_computation.56 | loop fusion | flops 12582912 | bytes 16626688 | tf_op jit(solution)/shard_map/sub | solution.py:47
  61.0 3.6 %collective-permute-done.4 = f32[3,1,64,256]{3,2,1,0:T(8,128)S(1)} collective-permute-done((f32[3,1,64,256]{3,2,1,0:T(8,128)S(1)}, f32[3,1,64,256]{3,2,1,0:T(8,128)S(1)}, u32[]{:S(2)}, u32[]{:S(2)}) %collective-permute-start.4) | collective-permute-done | bytes 196640 | tf_op jit(solution)/shard_map/ppermute | solution.py:28
  64.6 5.3 %collective-permute-done.5 = f32[3,1,64,256]{3,2,1,0:T(8,128)S(1)} collective-permute-done((f32[3,1,64,256]{3,2,1,0:T(8,128)S(1)}, f32[3,1,64,256]{3,2,1,0:T(8,128)S(1)}, u32[]{:S(2)}, u32[]{:S(2)}) %collective-permute-start.5) | collective-permute-done | bytes 196640 | tf_op jit(solution)/shard_map/ppermute | solution.py:26
  72.6 3.0 %collective-permute-done.7 = f32[3,18,1,256]{3,2,1,0:T(1,128)S(1)} collective-permute-done((f32[3,18,1,256]{3,2,1,0:T(1,128)S(1)}, f32[3,18,1,256]{3,2,1,0:T(1,128)S(1)}, u32[]{:S(2)}, u32[]{:S(2)}) %collective-permute-start.7) | collective-permute-done | bytes 55328 | tf_op jit(solution)/shard_map/ppermute | solution.py:26
  75.6 3.6 %select_maximum_fusion.4 = f32[3,18,66,258]{3,2,1,0:T(8,128)S(1)} fusion(f32[3,18,1,256]{3,2,1,0:T(1,128)S(1)} %collective-permute-done.6, f32[3,18,1,256]{3,2,1,0:T(1,128)S(1)} %collective-permute-done.7, f32[3,1,64,256]{3,2,1,0:T(8,128)S(1)} %collective-permute-done.4, f32[3,16,64,256]{3,2,1,0:T(8,128)S(1)} %fusion.19, ...), kind=kLoop, calls=%fused_computation.11 | loop fusion | flops 11034144 | bytes 7327584 | tf_op jit(solution)/shard_map/concatenate | solution.py:24
  79.2 3.5 %fusion.12 = f32[3,16,64,256]{3,2,1,0:T(8,128)S(1)} fusion(f32[3,16,64,256]{3,2,1,0:T(8,128)S(1)} %fusion.19, f32[3,18,66,258]{3,2,1,0:T(8,128)S(1)} %select_maximum_fusion.4, f32[3,1,64,256]{3,2,1,0:T(8,128)S(1)} %collective-permute-done.5, f32[3,1,64,256]{3,2,1,0:T(8,128)S(1)} %collective-permute-done.4, f32[3,18,1,256]{3,2,1,0:T(1,128)S(1)} %collective-permute-done.6, ...), kind=kLoop, calls=%fused_computation.39 | loop fusion | flops 15728640 | bytes 13087744 | tf_op jit(solution)/shard_map/sub | solution.py:47
  83.6 5.3 %collective-permute-start.21 = (f32[3,1,64,256]{3,2,1,0:T(8,128)}, f32[3,1,64,256]{3,2,1,0:T(8,128)S(1)}, u32[]{:S(2)}, u32[]{:S(2)}) collective-permute-start(f32[3,1,64,256]{3,2,1,0:T(8,128)} %get-tuple-element.18), channel_id=1, source_target_pairs={{1,0},{2,1},{3,2},{4,3},{5,4},{6,5},{7,6},{8,7},{9,8},{10,9},{11,1... | collective-permute-start | bytes 589832 | tf_op jit(solution)/shard_map/ppermute | solution.py:28
  101.6 3.7 %collective-permute-done.9 = f32[6,128]{1,0:T(8,128)S(1)} collective-permute-done((f32[6,128]{1,0:T(8,128)}, f32[6,128]{1,0:T(8,128)S(1)}, u32[]{:S(2)}, u32[]{:S(2)}) %collective-permute-start.9) | collective-permute-done | bytes 3104 | tf_op jit(solution)/shard_map/ppermute | solution.py:38
  110.1 3.6 %select_maximum_fusion = f32[3,18,66,258]{3,2,1,0:T(8,128)S(1)} fusion(f32[3,18,1,256]{3,2,1,0:T(1,128)S(1)} %collective-permute-done.22, f32[3,18,1,256]{3,2,1,0:T(1,128)S(1)} %collective-permute-done.23, f32[3,1,64,256]{3,2,1,0:T(8,128)S(1)} %collective-permute-done.21, f32[3,16,64,256]{3,2,1,0:T(8,128)S(1)} %fusion.12, ...), kind=kLoop, calls=%fused_computation.7 | loop fusion | flops 11034144 | bytes 7327584 | tf_op jit(solution)/shard_map/concatenate | solution.py:24
  114.9 3.2 %fusion.8 = (f32[3,1,16,64,256]{4,3,2,0,1:T(8,128)S(1)}, f32[3,1,16,64,256]{4,3,2,0,1:T(8,128)}) fusion(f32[3,18,1,256]{3,2,1,0:T(1,128)S(1)} %collective-permute-done.23, f32[3,1,64,256]{3,2,1,0:T(8,128)S(1)} %collective-permute-done.21, f32[3,16,64,256]{3,2,1,0:T(8,128)S(1)} %fusion.12, f32[3,1,64,256]{3,2,1,0:T(8,128)S(1)} %collective-permute-done.20, ...), kind=kLoop, calls=%fused_computation.29 | loop fusion | flops 9437184 | bytes 9940992 | tf_op jit(solution)/shard_map/stack | solution.py:54
  120.7 4.8 %copy.137 = f32[3,3,16,64,256]{4,3,2,1,0:T(8,128)} copy(f32[3,3,16,64,256]{4,3,2,0,1:T(8,128)S(1)} %pad_maximum_fusion) | data formatting | bytes 18874368 | tf_op jit(solution)/shard_map/stack | solution.py:54
  125.5 10.8 %reshape.53 = f32[9,2048,128]{2,1,0:T(8,128)} reshape(f32[3,3,16,64,256]{4,3,2,1,0:T(8,128)} %copy.137) | data formatting | bytes 18874368 | tf_op jit(solution)/shard_map/reshape | solution.py:124
  136.3 12.7 %copy.138 = f32[9,2048,128]{2,0,1:T(8,128)} copy(f32[9,2048,128]{2,1,0:T(8,128)} %reshape.53) | data formatting | bytes 18874368 | tf_op jit(solution)/shard_map/reshape | solution.py:124
  149.0 6.5 %gather_fusion = f32[192,9,128]{2,1,0:T(8,128)S(1)} fusion(f32[9,2048,128]{2,0,1:T(8,128)} %copy.138, s32[1024]{0:T(1024)S(1)} %pad_clamp_fusion), kind=kCustom, calls=%fused_computation | custom fusion | bytes 1770240 | tf_op jit(solution)/shard_map/jit(_take)/gather | solution.py:66
  157.3 20.3 %scatter_fusion = f32[9,256,128]{2,0,1:T(8,128)} fusion(f32[9,256,128]{2,0,1:T(8,128)} %broadcast_in_dim.39, s32[192]{0:T(256)S(1)} %bitcast.56, f32[192,9,128]{2,1,0:T(8,128)S(1)} %broadcast_select_fusion), kind=kCustom, calls=%fused_computation.3 | custom fusion | bytes 2654976 | tf_op jit(solution)/shard_map/scatter | solution.py:68
  177.6 7.6 %all-to-all-start = ((f32[9,256,128]{2,0,1:T(8,128)}), f32[9,256,128]{2,0,1:T(8,128)S(1)}, u32[]{:S(2)}, u32[]{:S(2)}) async-start(f32[9,256,128]{2,0,1:T(8,128)} %scatter_fusion), calls=%async_computation | async-start | bytes 4194304 | tf_op jit(solution)/shard_map/all_to_all | solution.py:126
  188.3 21.3 %collective-permute-done.18 = f32[6,128]{1,0:T(8,128)S(1)} collective-permute-done((f32[6,128]{1,0:T(8,128)S(1)}, f32[6,128]{1,0:T(8,128)S(1)}, u32[]{:S(2)}, u32[]{:S(2)}) %collective-permute-start.18) | collective-permute-done | bytes 3104 | tf_op jit(solution)/shard_map/ppermute | solution.py:38
  209.6 5.8 %collective-permute-start.16 = (f32[6,128]{1,0:T(8,128)}, f32[6,128]{1,0:T(8,128)S(1)}, u32[]{:S(2)}, u32[]{:S(2)}) collective-permute-start(f32[6,128]{1,0:T(8,128)} %collective-permute-done.15), channel_id=1, source_target_pairs={{1,0},{2,1},{3,2},{4,3},{5,4},{6,5},{7,6},{8,7},{9,8},{10,9},{11,1... | collective-permute-start | bytes 9224 | tf_op jit(solution)/shard_map/ppermute | solution.py:38
  216.9 5.4 %collective-permute-done.19 = f32[6,128]{1,0:T(8,128)S(1)} collective-permute-done((f32[6,128]{1,0:T(8,128)S(1)}, f32[6,128]{1,0:T(8,128)S(1)}, u32[]{:S(2)}, u32[]{:S(2)}) %collective-permute-start.19) | collective-permute-done | bytes 3104 | tf_op jit(solution)/shard_map/ppermute | solution.py:38
  222.3 8.9 %copy.142 = f32[9,256,128]{0,2,1:T(8,128)} copy(f32[9,256,128]{2,0,1:T(8,128)S(1)} %all-to-all-done) | data formatting | bytes 2359296 | tf_op jit(solution)/shard_map/reshape | solution.py:127
  231.2 19.2 %gather_fusion.1 = f32[5120,9]{1,0:T(8,128)S(1)} fusion(f32[9,32768]{0,1:T(8,128)} %bitcast.39, s32[5120]{0:T(1024)S(1)} %copy-done.6), kind=kCustom, calls=%fused_computation.1 | custom fusion | bytes 389120 | tf_op jit(solution)/shard_map/jit(_take)/gather | solution.py:140
  (130 shorter events, 68.5 us)
Async XLA Ops:
  2.5 42.5 %collective-permute-start.1 = (f32[3,1,64,256]{3,2,1,0:T(8,128)}, f32[3,1,64,256]{3,2,1,0:T(8,128)S(1)}, u32[]{:S(2)}, u32[]{:S(2)}) collective-permute-start(f32[3,1,64,256]{3,2,1,0:T(8,128)} %get-tuple-element.23), channel_id=1, source_target_pairs={{0,1},{1,2},{2,3},{3,4},{4,5},{5,6},{6,7},{7,8},{8,9},{9,10},{10,1... | collective-permute-start | bytes 589832 | tf_op jit(solution)/shard_map/ppermute | solution.py:26
  4.5 40.9 %collective-permute-start = (f32[3,1,64,256]{3,2,1,0:T(8,128)}, f32[3,1,64,256]{3,2,1,0:T(8,128)S(1)}, u32[]{:S(2)}, u32[]{:S(2)}) collective-permute-start(f32[3,1,64,256]{3,2,1,0:T(8,128)} %get-tuple-element.22), channel_id=1, source_target_pairs={{1,0},{2,1},{3,2},{4,3},{5,4},{6,5},{7,6},{8,7},{9,8},{10,9},{11,1... | collective-permute-start | bytes 589832 | tf_op jit(solution)/shard_map/ppermute | solution.py:28
  33.7 67.7 %collective-permute-start.8 = (f32[6,128]{1,0:T(8,128)}, f32[6,128]{1,0:T(8,128)}, u32[]{:S(2)}, u32[]{:S(2)}) collective-permute-start(f32[6,128]{1,0:T(8,128)} %copy.144), channel_id=1, source_target_pairs={{16,0},{32,16},{48,32},{64,48},{80,64},{96,80},{112,96},{0,112},{1... | collective-permute-start | bytes 9224 | tf_op jit(solution)/shard_map/ppermute | solution.py:38
  37.1 148.1 %collective-permute-start.10 = (f32[6,128]{1,0:T(8,128)}, f32[6,128]{1,0:T(8,128)}, u32[]{:S(2)}, u32[]{:S(2)}) collective-permute-start(f32[6,128]{1,0:T(8,128)} %copy.145), channel_id=1, source_target_pairs={{16,0},{32,16},{48,32},{64,48},{80,64},{96,80},{112,96},{0,112},{1... | collective-permute-start | bytes 9224 | tf_op jit(solution)/shard_map/ppermute | solution.py:38
  39.6 145.7 %collective-permute-start.11 = (f32[6,128]{1,0:T(8,128)}, f32[6,128]{1,0:T(8,128)}, u32[]{:S(2)}, u32[]{:S(2)}) collective-permute-start(f32[6,128]{1,0:T(8,128)} %copy.146), channel_id=1, source_target_pairs={{16,0},{32,16},{48,32},{64,48},{80,64},{96,80},{112,96},{0,112},{1... | collective-permute-start | bytes 9224 | tf_op jit(solution)/shard_map/ppermute | solution.py:38
  45.4 2.8 %collective-permute-start.2 = (f32[3,18,1,256]{3,2,1,0:T(1,128)S(1)}, f32[3,18,1,256]{3,2,1,0:T(1,128)S(1)}, u32[]{:S(2)}, u32[]{:S(2)}) collective-permute-start(f32[3,18,1,256]{3,2,1,0:T(1,128)S(1)} %get-tuple-element.17), channel_id=1, source_target_pairs={{16,0},{32,16},{48,32},{64,48},{80,64},{96,80},{112,96},{0,112},{1... | collective-permute-start | bytes 165896 | tf_op jit(solution)/shard_map/ppermute | solution.py:28
  46.4 4.8 %collective-permute-start.3 = (f32[3,18,1,256]{3,2,1,0:T(1,128)S(1)}, f32[3,18,1,256]{3,2,1,0:T(1,128)S(1)}, u32[]{:S(2)}, u32[]{:S(2)}) collective-permute-start(f32[3,18,1,256]{3,2,1,0:T(1,128)S(1)} %get-tuple-element.16), channel_id=1, source_target_pairs={{0,16},{16,32},{32,48},{48,64},{64,80},{80,96},{96,112},{112,0},{1... | collective-permute-start | bytes 165896 | tf_op jit(solution)/shard_map/ppermute | solution.py:26
  58.9 5.7 %collective-permute-start.4 = (f32[3,1,64,256]{3,2,1,0:T(8,128)S(1)}, f32[3,1,64,256]{3,2,1,0:T(8,128)S(1)}, u32[]{:S(2)}, u32[]{:S(2)}) collective-permute-start(f32[3,1,64,256]{3,2,1,0:T(8,128)S(1)} %get-tuple-element.21), channel_id=1, source_target_pairs={{1,0},{2,1},{3,2},{4,3},{5,4},{6,5},{7,6},{8,7},{9,8},{10,9},{11,1... | collective-permute-start | bytes 589832 | tf_op jit(solution)/shard_map/ppermute | solution.py:28
  60.9 9.0 %collective-permute-start.5 = (f32[3,1,64,256]{3,2,1,0:T(8,128)S(1)}, f32[3,1,64,256]{3,2,1,0:T(8,128)S(1)}, u32[]{:S(2)}, u32[]{:S(2)}) collective-permute-start(f32[3,1,64,256]{3,2,1,0:T(8,128)S(1)} %get-tuple-element.20), channel_id=1, source_target_pairs={{0,1},{1,2},{2,3},{3,4},{4,5},{5,6},{6,7},{7,8},{8,9},{9,10},{10,1... | collective-permute-start | bytes 589832 | tf_op jit(solution)/shard_map/ppermute | solution.py:26
  70.8 4.8 %collective-permute-start.7 = (f32[3,18,1,256]{3,2,1,0:T(1,128)S(1)}, f32[3,18,1,256]{3,2,1,0:T(1,128)S(1)}, u32[]{:S(2)}, u32[]{:S(2)}) collective-permute-start(f32[3,18,1,256]{3,2,1,0:T(1,128)S(1)} %get-tuple-element.14), channel_id=1, source_target_pairs={{0,16},{16,32},{32,48},{48,64},{64,80},{80,96},{96,112},{112,0},{1... | collective-permute-start | bytes 165896 | tf_op jit(solution)/shard_map/ppermute | solution.py:26
  83.6 17.8 %collective-permute-start.20 = (f32[3,1,64,256]{3,2,1,0:T(8,128)}, f32[3,1,64,256]{3,2,1,0:T(8,128)S(1)}, u32[]{:S(2)}, u32[]{:S(2)}) collective-permute-start(f32[3,1,64,256]{3,2,1,0:T(8,128)} %get-tuple-element.19), channel_id=1, source_target_pairs={{0,1},{1,2},{2,3},{3,4},{4,5},{5,6},{6,7},{7,8},{8,9},{9,10},{10,1... | collective-permute-start | bytes 589832 | tf_op jit(solution)/shard_map/ppermute | solution.py:26
  83.6 17.9 %collective-permute-start.21 = (f32[3,1,64,256]{3,2,1,0:T(8,128)}, f32[3,1,64,256]{3,2,1,0:T(8,128)S(1)}, u32[]{:S(2)}, u32[]{:S(2)}) collective-permute-start(f32[3,1,64,256]{3,2,1,0:T(8,128)} %get-tuple-element.18), channel_id=1, source_target_pairs={{1,0},{2,1},{3,2},{4,3},{5,4},{6,5},{7,6},{8,7},{9,8},{10,9},{11,1... | collective-permute-start | bytes 589832 | tf_op jit(solution)/shard_map/ppermute | solution.py:28
  101.4 114.0 %collective-permute-start.13 = (f32[6,128]{1,0:T(8,128)}, f32[6,128]{1,0:T(8,128)}, u32[]{:S(2)}, u32[]{:S(2)}) collective-permute-start(f32[6,128]{1,0:T(8,128)} %copy.147), channel_id=1, source_target_pairs={{1,0},{2,1},{3,2},{4,3},{5,4},{6,5},{7,6},{8,7},{9,8},{10,9},{11,1... | collective-permute-start | bytes 9224 | tf_op jit(solution)/shard_map/ppermute | solution.py:38
  101.4 3.9 %collective-permute-start.9 = (f32[6,128]{1,0:T(8,128)}, f32[6,128]{1,0:T(8,128)S(1)}, u32[]{:S(2)}, u32[]{:S(2)}) collective-permute-start(f32[6,128]{1,0:T(8,128)} %collective-permute-done.8), channel_id=1, source_target_pairs={{1,0},{2,1},{3,2},{4,3},{5,4},{6,5},{7,6},{8,7},{9,8},{10,9},{11,1... | collective-permute-start | bytes 9224 | tf_op jit(solution)/shard_map/ppermute | solution.py:38
  101.6 4.3 %collective-permute-start.22 = (f32[3,18,1,256]{3,2,1,0:T(1,128)S(1)}, f32[3,18,1,256]{3,2,1,0:T(1,128)S(1)}, u32[]{:S(2)}, u32[]{:S(2)}) collective-permute-start(f32[3,18,1,256]{3,2,1,0:T(1,128)S(1)} %get-tuple-element.13), channel_id=1, source_target_pairs={{16,0},{32,16},{48,32},{64,48},{80,64},{96,80},{112,96},{0,112},{1... | collective-permute-start | bytes 165896 | tf_op jit(solution)/shard_map/ppermute | solution.py:28
  105.3 4.8 %collective-permute-start.23 = (f32[3,18,1,256]{3,2,1,0:T(1,128)S(1)}, f32[3,18,1,256]{3,2,1,0:T(1,128)S(1)}, u32[]{:S(2)}, u32[]{:S(2)}) collective-permute-start(f32[3,18,1,256]{3,2,1,0:T(1,128)S(1)} %get-tuple-element.12), channel_id=1, source_target_pairs={{0,16},{16,32},{32,48},{48,64},{64,80},{80,96},{96,112},{112,0},{1... | collective-permute-start | bytes 165896 | tf_op jit(solution)/shard_map/ppermute | solution.py:26
  106.0 110.1 %collective-permute-start.14 = (f32[6,128]{1,0:T(8,128)}, f32[6,128]{1,0:T(8,128)}, u32[]{:S(2)}, u32[]{:S(2)}) collective-permute-start(f32[6,128]{1,0:T(8,128)} %copy.149), channel_id=1, source_target_pairs={{15,0},{0,1},{1,2},{2,3},{3,4},{4,5},{5,6},{6,7},{7,8},{8,9},{9,10... | collective-permute-start | bytes 9224 | tf_op jit(solution)/shard_map/ppermute | solution.py:38
  110.1 77.0 %collective-permute-start.15 = (f32[6,128]{1,0:T(8,128)}, f32[6,128]{1,0:T(8,128)}, u32[]{:S(2)}, u32[]{:S(2)}) collective-permute-start(f32[6,128]{1,0:T(8,128)} %copy.150), channel_id=1, source_target_pairs={{112,0},{0,16},{16,32},{32,48},{48,64},{64,80},{80,96},{96,112},{1... | collective-permute-start | bytes 9224 | tf_op jit(solution)/shard_map/ppermute | solution.py:38
  177.6 44.8 %all-to-all-start = ((f32[9,256,128]{2,0,1:T(8,128)}), f32[9,256,128]{2,0,1:T(8,128)S(1)}, u32[]{:S(2)}, u32[]{:S(2)}) async-start(f32[9,256,128]{2,0,1:T(8,128)} %scatter_fusion), calls=%async_computation | async-start | bytes 4194304 | tf_op jit(solution)/shard_map/all_to_all | solution.py:126
  185.2 24.4 %collective-permute-start.18 = (f32[6,128]{1,0:T(8,128)S(1)}, f32[6,128]{1,0:T(8,128)S(1)}, u32[]{:S(2)}, u32[]{:S(2)}) collective-permute-start(f32[6,128]{1,0:T(8,128)S(1)} %copy-done.9), channel_id=1, source_target_pairs={{112,0},{0,16},{16,32},{32,48},{48,64},{64,80},{80,96},{96,112},{1... | collective-permute-start | bytes 9224 | tf_op jit(solution)/shard_map/ppermute | solution.py:38
  185.3 30.1 %collective-permute-start.12 = (f32[6,128]{1,0:T(8,128)}, f32[6,128]{1,0:T(8,128)S(1)}, u32[]{:S(2)}, u32[]{:S(2)}) collective-permute-start(f32[6,128]{1,0:T(8,128)} %collective-permute-done.11), channel_id=1, source_target_pairs={{15,0},{0,1},{1,2},{2,3},{3,4},{4,5},{5,6},{6,7},{7,8},{8,9},{9,10... | collective-permute-start | bytes 9224 | tf_op jit(solution)/shard_map/ppermute | solution.py:38
  187.2 29.8 %collective-permute-start.17 = (f32[6,128]{1,0:T(8,128)S(1)}, f32[6,128]{1,0:T(8,128)S(1)}, u32[]{:S(2)}, u32[]{:S(2)}) collective-permute-start(f32[6,128]{1,0:T(8,128)S(1)} %copy-done.8), channel_id=1, source_target_pairs={{112,0},{0,16},{16,32},{32,48},{48,64},{64,80},{80,96},{96,112},{1... | collective-permute-start | bytes 9224 | tf_op jit(solution)/shard_map/ppermute | solution.py:38
  209.6 7.3 %collective-permute-start.16 = (f32[6,128]{1,0:T(8,128)}, f32[6,128]{1,0:T(8,128)S(1)}, u32[]{:S(2)}, u32[]{:S(2)}) collective-permute-start(f32[6,128]{1,0:T(8,128)} %collective-permute-done.15), channel_id=1, source_target_pairs={{1,0},{2,1},{3,2},{4,3},{5,4},{6,5},{7,6},{8,7},{9,8},{10,9},{11,1... | collective-permute-start | bytes 9224 | tf_op jit(solution)/shard_map/ppermute | solution.py:38
  215.4 6.9 %collective-permute-start.19 = (f32[6,128]{1,0:T(8,128)S(1)}, f32[6,128]{1,0:T(8,128)S(1)}, u32[]{:S(2)}, u32[]{:S(2)}) collective-permute-start(f32[6,128]{1,0:T(8,128)S(1)} %collective-permute-done.18), channel_id=1, source_target_pairs={{15,0},{0,1},{1,2},{2,3},{3,4},{4,5},{5,6},{6,7},{7,8},{8,9},{9,10... | collective-permute-start | bytes 9224 | tf_op jit(solution)/shard_map/ppermute | solution.py:38
  (13 other events, 260.4 us)
where the time goes:
time: 255 us; the launch traced here: 253 us
  local copies, waits for them, and re-layouts  126 us (49%)
  waiting for transfers between devices  51.1 us (20%)
  other arithmetic  37.6 us (15%)
  starting transfers between devices  36.5 us (14%)
    ppermute x12, waiting for transfers between devices, from_behind(): return lax.ppermute(block, axis, route)  30.5 us
    reshape x2, local copies, waits for them, and re-layouts, per_device(): row_table = grads.reshape(9, row_count, 128)  23.5 us
    unnamed x47, local copies, waits for them, and re-layouts  21.7 us
    scatter x1, local copies, waits for them, and re-layouts, pack_rows(): return empty.at[:, slot_pos].set(picked)  20.3 us
    gather x2, local copies, waits for them, and re-layouts, per_device(): tensor = jnp.take(flat_table, fibre_cell, axis=1)  20 us
    ppermute x6, starting transfers between devices, extended(): lax.ppermute(head, axis, [((i + 1) % count, i) for i in range(count)])  13.8 us
    ppermute x6, waiting for transfers between devices, extended(): lax.ppermute(tail, axis, [(i, (i + 1) % count) for i in range(count)])  13.6 us
    ppermute x12, starting transfers between devices, from_behind(): return lax.ppermute(block, axis, route)  13.1 us
  transfers between devices with their start and end apart: 25, of which 11 were waited for; matrix products, arithmetic and copies ran while one was open for 52% of the time, Pallas kernels for 0%

commit v1 on v0

v1 whole, which is shorter than its diff:
```python
import functools

import jax
import jax.numpy as jnp
from jax import lax
from jax.experimental import pallas as pl
from jax.experimental.pallas import tpu as pltpu
from jax.sharding import PartitionSpec as P

FIB_DEV = 4096
CAP = 128
SLOT_DEV = 5120
RCAP = 2
CX, CZ, NY = 64, 16, 256
XW = 72
ROWS = 2048

DIFFUSION = 0.1
ADVECTION = 0.4
SHAPE_FACTOR = 0.9
TURN_STEP = 0.25

MESH = pl.DeviceIdType.MESH
F32 = jnp.float32
BF16 = jnp.bfloat16
I32 = jnp.int32
MIB = 2**20


def code_offset(code):
    return code * CAP if code <= 4 else FIB_DEV + (code - 1) * CAP


def place(device, gz_size):
    return (device // gz_size, lax.rem(device, gz_size))


def split3(x):
    hi = x.astype(BF16).astype(F32)
    mid = (x - hi).astype(BF16).astype(F32)
    return hi, mid, x - hi - mid


def iota(shape, dim):
    return lax.broadcasted_iota(I32, shape, dim)


def slot_list(rows_ref, readers_ref):
    n = rows_ref.shape[1]
    rows, readers = rows_ref[...], readers_ref[...]
    sub, lane = iota((n, n), 0), iota((n, n), 1)
    diag = sub == lane

    def column(row):
        return jnp.sum(jnp.where(diag, jnp.broadcast_to(row, (n, n)), 0), axis=1, keepdims=True)

    same = (column(readers) == readers) & (sub < lane)
    rank = jnp.sum(same.astype(I32), axis=0, keepdims=True)
    slot = column(readers * RCAP + rank)
    table_row = column(((rows // 128) * 2 + rows % 2) * CX + (rows // 2) % CX)
    slots = iota((n, 256), 1)
    return jnp.sum(jnp.where(slot == slots, table_row - ROWS, 0), axis=0, keepdims=True) + ROWS


def fibre_ranks(code):
    masks = [code == c for c in range(9)]
    ones = jnp.concatenate([m.astype(F32) for m in masks], axis=0).astype(BF16)
    tri = (iota((128, 128), 0) < iota((128, 128), 1)).astype(BF16)
    before = jnp.dot(ones, tri, preferred_element_type=F32)
    total = jnp.dot(ones, jnp.ones((128, 128), BF16), preferred_element_type=F32)
    low = (iota((32, 32), 1) < iota((32, 32), 0)).astype(BF16)
    rank = jnp.zeros((32, 128), F32)
    for c in range(9):
        part = total[32 * c : 32 * c + 32]
        above = jnp.dot(low, part.astype(BF16), preferred_element_type=F32)
        rank = jnp.where(masks[c], before[32 * c : 32 * c + 32] + above, rank)
        if c == 4:
            stay = jnp.sum(part, axis=0, keepdims=True)[:, 0:1]
    return rank.astype(I32), stay.astype(I32)


def as_row(x):
    return jnp.concatenate([x[r : r + 1] for r in range(x.shape[0])], axis=1)


def compact(records, shift, stay):
    shape = records.shape
    n = shape[1]
    for b in range(11):
        w = 1 << b
        came_shift = pltpu.roll(shift, n - w, 1)
        came = pltpu.roll(records, n - w, 1)
        arrive = (came_shift & w) != 0
        leave = (shift & w) != 0
        records = jnp.where(arrive, came, records)
        shift = jnp.where(arrive, came_shift, jnp.where(leave, 0, shift))
    return jnp.where(iota(shape, 1) < stay, records, 0.0)


def pack_fibres(fibres_ref, code_ref, split_ref, pieces_ref, arrived_ref):
    code = code_ref[...]
    rank, stay = fibre_ranks(code)
    fibre = iota((32, 128), 0) * 128 + iota((32, 128), 1)
    shift = as_row(jnp.where(code == 4, fibre - rank, 0))
    slot = as_row(jnp.where(code == 4, -1, jnp.where(code < 4, code, code - 1) * CAP + rank))
    split_ref[...] = jnp.zeros(split_ref.shape, F32)
    for i, part in enumerate(split3(fibres_ref[...])):
        split_ref[8 * i : 8 * i + 6, :] = part
    acc = jnp.zeros((24, 8 * CAP), F32)
    step = 512
    for k in range(FIB_DEV // step):
        onehot = (iota((8 * CAP, step), 0) == slot[:, k * step : k * step + step]).astype(F32).astype(BF16)
        acc = acc + lax.dot_general(
            split_ref[:, k * step : k * step + step].astype(BF16),
            onehot,
            (((1,), (1,)), ((), ())),
            preferred_element_type=F32,
        )
    packed = acc[0:6] + acc[8:14] + acc[16:22]
    for j in range(8):
        pieces_ref[j] = packed[:, j * CAP : j * CAP + CAP]
    records = fibres_ref[...]
    arrived_ref[:, 4 * CAP : 4 * CAP + FIB_DEV] = compact(records, jnp.broadcast_to(shift, records.shape), stay)


def halo_kernel(
    sizes, velocity, fibres, code, rows, readers,
    zlo, zhi, xlo, xhi, corner, arrived, slots,
    split, pieces, halo_send, halo_recv, fib_send, fib_recv,
):
    nx, nz = sizes
    ix, iz = lax.axis_index("gx"), lax.axis_index("gz")

    def at(dx, dz):
        return (lax.rem(ix + dx + nx, nx), lax.rem(iz + dz + nz, nz))

    around = [(dx, dz) for dx in (-1, 0, 1) for dz in (-1, 0, 1) if (dx, dz) != (0, 0)]
    barrier = pltpu.get_barrier_semaphore()
    for dx, dz in around:
        pl.semaphore_signal(barrier, inc=1, device_id=at(dx, dz), device_id_type=MESH)
    pl.semaphore_wait(barrier, 8)

    copies = []

    def send(src, dst, dx, dz):
        i = len(copies)
        copy = pltpu.make_async_remote_copy(
            src, dst, halo_send.at[i], halo_recv.at[i], device_id=at(dx, dz), device_id_type=MESH
        )
        copy.start()
        copies.append(copy)

    send(velocity.at[:, 13:16], zlo, 0, 1)
    send(velocity.at[:, 0:3], zhi, 0, -1)
    send(velocity.at[:, :, 56:64], xlo, 1, 0)
    send(velocity.at[:, :, 0:8], xhi, -1, 0)
    send(velocity.at[:, 14:16, 56:64], corner.at[0], 1, 1)
    send(velocity.at[:, 14:16, 0:8], corner.at[1], -1, 1)
    send(velocity.at[:, 0:2, 56:64], corner.at[2], 1, -1)
    send(velocity.at[:, 0:2, 0:8], corner.at[3], -1, -1)

    pack_fibres(fibres, code, split, pieces, arrived)
    moved = []
    for j, (dx, dz) in enumerate(around):
        off = code_offset((dx + 1) * 3 + dz + 1)
        copy = pltpu.make_async_remote_copy(
            pieces.at[j], arrived.at[:, off : off + CAP], fib_send.at[j], fib_recv.at[j],
            device_id=at(dx, dz), device_id_type=MESH,
        )
        copy.start()
        moved.append(copy)
    slots[...] = slot_list(rows, readers)
    for copy in copies + moved:
        copy.wait()


def any_spec():
    return pl.BlockSpec(memory_space=pl.ANY)


def vmem_spec():
    return pl.BlockSpec(memory_space=pltpu.VMEM)


def halo_call(sizes, velocity, fibres, code, rows, readers):
    return pl.pallas_call(
        functools.partial(halo_kernel, sizes),
        out_shape=(
            jax.ShapeDtypeStruct((3, 3, CX, NY), F32),
            jax.ShapeDtypeStruct((3, 3, CX, NY), F32),
            jax.ShapeDtypeStruct((3, CZ, 8, NY), F32),
            jax.ShapeDtypeStruct((3, CZ, 8, NY), F32),
            jax.ShapeDtypeStruct((4, 3, 2, 8, NY), F32),
            jax.ShapeDtypeStruct((6, SLOT_DEV), F32),
            jax.ShapeDtypeStruct((1, 256), I32),
        ),
        in_specs=[any_spec()] + [vmem_spec()] * 4,
        out_specs=(any_spec(),) * 5 + (vmem_spec(),) * 2,
        scratch_shapes=[
            pltpu.VMEM((24, FIB_DEV), F32),
            pltpu.VMEM((8, 6, CAP), F32),
            pltpu.SemaphoreType.DMA((8,)),
            pltpu.SemaphoreType.DMA((8,)),
            pltpu.SemaphoreType.DMA((8,)),
            pltpu.SemaphoreType.DMA((8,)),
        ],
        compiler_params=pltpu.CompilerParams(
            collective_id=0, has_side_effects=True, vmem_limit_bytes=40 * MIB
        ),
        name="halo_and_fibres",
    )(velocity, fibres, code, rows, readers)


def beside(plane):
    lane = iota(plane.shape, 1)
    xp = pltpu.roll(plane, XW - 1, 0)
    xm = pltpu.roll(plane, 1, 0)
    yp = jnp.where(lane == NY - 1, 0.0, pltpu.roll(plane, NY - 1, 1))
    ym = jnp.where(lane == 0, 0.0, pltpu.roll(plane, 1, 1))
    return xp, xm, yp, ym


def transport_kernel(slots, velocity, zlo, zhi, xlo, xhi, corner, flow, out, send, first, second, third, grads):
    first[3:19, 0:64, :] = velocity[0]
    first[0:3, 0:64, :] = zlo[0]
    first[19:22, 0:64, :] = zhi[0]
    sub = iota((1, 8, NY), 1) < 4
    first[3:19, 64:72, :] = jnp.where(sub, xhi[0], xlo[0])
    first[1:3, 64:72, :] = jnp.where(sub, corner[1, 0], corner[0, 0])
    first[19:21, 64:72, :] = jnp.where(sub, corner[3, 0], corner[2, 0])

    ahead = DIFFUSION - 0.5 * ADVECTION * flow[...]
    behind = DIFFUSION + 0.5 * ADVECTION * flow[...]

    def advance(old, new, count):
        @pl.loop(0, count)
        def _(z):
            centre = old[z + 1]
            xp, xm, yp, ym = beside(centre)
            near = old[z] + old[z + 2] + yp + ym
            new[z] = (1.0 - 6.0 * DIFFUSION) * centre + DIFFUSION * near + ahead * xp + behind * xm

    advance(first, second, 20)
    advance(second, third, 18)
    grads[:, ROWS : ROWS + 8, :] = jnp.zeros((3, 8, 128), F32)

    @pl.loop(0, CZ)
    def _(z):
        centre = third[z + 1]
        out[0, z] = centre[0:64]
        xp, xm, yp, ym = beside(centre)
        along_z = third[z + 2] - third[z]
        for j, d in enumerate((xp - xm, yp - ym, along_z)):
            d = 0.5 * d
            for h in range(2):
                base = pl.multiple_of((z * 2 + h) * CX, CX)
                grads[j, pl.ds(base, CX), :] = d[0:64, h * 128 : h * 128 + 128]

    @pl.loop(0, 32)
    def _(g):
        base = pl.multiple_of(g * 8, 8)
        for k in range(8):
            row = slots[0, base + k]
            for j in range(3):
                send[j, pl.ds(base + k, 1), :] = grads[j, pl.ds(row, 1), :]


def transport_call(slots, velocity, zlo, zhi, xlo, xhi, corner, flow):
    return pl.pallas_call(
        transport_kernel,
        grid=(3,),
        out_shape=(
            jax.ShapeDtypeStruct((3, CZ, CX, NY), F32),
            jax.ShapeDtypeStruct((9, 256, 128), F32),
        ),
        in_specs=[
            pl.BlockSpec(memory_space=pltpu.SMEM),
            pl.BlockSpec((1, CZ, CX, NY), lambda c: (c, 0, 0, 0)),
            pl.BlockSpec((1, 3, CX, NY), lambda c: (c, 0, 0, 0)),
            pl.BlockSpec((1, 3, CX, NY), lambda c: (c, 0, 0, 0)),
            pl.BlockSpec((1, CZ, 8, NY), lambda c: (c, 0, 0, 0)),
            pl.BlockSpec((1, CZ, 8, NY), lambda c: (c, 0, 0, 0)),
            pl.BlockSpec((4, 1, 2, 8, NY), lambda c: (0, c, 0, 0, 0)),
            pl.BlockSpec((1, NY), lambda c: (0, 0)),
        ],
        out_specs=(
            pl.BlockSpec((1, CZ, CX, NY), lambda c: (c, 0, 0, 0)),
            pl.BlockSpec((3, 256, 128), lambda c: (c, 0, 0)),
        ),
        scratch_shapes=[
            pltpu.VMEM((22, XW, NY), F32),
            pltpu.VMEM((20, XW, NY), F32),
            pltpu.VMEM((18, XW, NY), F32),
            pltpu.VMEM((3, ROWS + 8, 128), F32),
        ],
        compiler_params=pltpu.CompilerParams(vmem_limit_bytes=40 * MIB),
        name="transport_and_rows",
    )(slots, velocity, zlo, zhi, xlo, xhi, corner, flow)


def exchange_kernel(sizes, send, recv, send_sem, recv_sem, own_sem):
    nx, nz = sizes
    count = nx * nz
    me = lax.axis_index("gx") * nz + lax.axis_index("gz")
    barrier = pltpu.get_barrier_semaphore()

    @pl.loop(1, count)
    def _(i):
        there = place(lax.rem(me + i, count), nz)
        pl.semaphore_signal(barrier, inc=1, device_id=there, device_id_type=MESH)

    pl.semaphore_wait(barrier, count - 1)
    own = pltpu.make_async_copy(send.at[:, me], recv.at[:, me], own_sem)
    own.start()

    @pl.loop(1, count)
    def _(i):
        reader = lax.rem(me + i, count)
        pltpu.make_async_remote_copy(
            send.at[:, reader], recv.at[:, me], send_sem, recv_sem,
            device_id=place(reader, nz), device_id_type=MESH,
        ).start()

    others = pl.ds(0, count - 1)
    pltpu.make_async_copy(recv.at[:, others], recv.at[:, others], recv_sem).wait()
    pltpu.make_async_copy(send.at[:, others], send.at[:, others], send_sem).wait()
    own.wait()


def exchange_call(sizes, send):
    return pl.pallas_call(
        functools.partial(exchange_kernel, sizes),
        out_shape=jax.ShapeDtypeStruct(send.shape, F32),
        in_specs=[any_spec()],
        out_specs=any_spec(),
        scratch_shapes=[pltpu.SemaphoreType.DMA] * 3,
        compiler_params=pltpu.CompilerParams(collective_id=1, has_side_effects=True),
        name="row_exchange",
    )(send)


def jeffery(orient, tensor):
    along = [sum(tensor[3 * i + j] * orient[j] for j in range(3)) for i in range(3)]
    across = [sum(tensor[3 * j + i] * orient[j] for j in range(3)) for i in range(3)]
    stretch = sum(orient[i] * along[i] for i in range(3))
    turned = []
    for i in range(3):
        strain = 0.5 * (along[i] + across[i])
        rotation = 0.5 * (along[i] - across[i])
        turned.append(orient[i] + TURN_STEP * (rotation + SHAPE_FACTOR * (strain - stretch * orient[i])))
    return turned


def turn_kernel(recv, cell, arrived, out, table):
    for q in range(9):
        block = jnp.transpose(recv[q])
        hi = block.astype(BF16)
        table[128 * q : 128 * q + 128, 0:256] = hi
        table[128 * q : 128 * q + 128, 256:512] = (block - hi.astype(F32)).astype(BF16)
    width = 256

    @pl.loop(0, SLOT_DEV // width)
    def _(k):
        base = pl.multiple_of(k * width, width)
        here = cell[:, pl.ds(base, width)]
        onehot = (iota((256, width), 0) == here // 128).astype(F32).astype(BF16)
        picked = jnp.dot(table[...], jnp.concatenate([onehot, onehot], axis=0), preferred_element_type=F32)
        lane = iota((128, width), 0) == here % 128
        tensor = [
            jnp.sum(jnp.where(lane, picked[128 * q : 128 * q + 128], 0.0), axis=0, keepdims=True) for q in range(9)
        ]
        records = arrived[:, pl.ds(base, width)]
        turned = jeffery([records[3 + i : 4 + i] for i in range(3)], tensor)
        out[0:3, pl.ds(base, width)] = records[0:3]
        for i in range(3):
            out[3 + i : 4 + i, pl.ds(base, width)] = turned[i]


def turn_call(recv, cell, arrived):
    return pl.pallas_call(
        turn_kernel,
        out_shape=jax.ShapeDtypeStruct((6, SLOT_DEV), F32),
        in_specs=[vmem_spec()] * 3,
        out_specs=vmem_spec(),
        scratch_shapes=[pltpu.VMEM((1152, 512), BF16)],
        compiler_params=pltpu.CompilerParams(vmem_limit_bytes=40 * MIB),
        name="gather_and_turn",
    )(recv, cell, arrived)


def per_device(sizes, velocity, mean_flow, fibres, moves, grad_rows, grad_readers, fibre_cell):
    count = sizes[0] * sizes[1]
    zlo, zhi, xlo, xhi, corner, arrived, slots = halo_call(
        sizes, velocity, fibres, moves.reshape(32, 128), grad_rows.reshape(1, -1), grad_readers.reshape(1, -1)
    )
    flow, send = transport_call(slots, velocity, zlo, zhi, xlo, xhi, corner, mean_flow.reshape(1, NY))
    recv = exchange_call(sizes, send.reshape(9, count, RCAP, 128))
    out = turn_call(recv.reshape(9, count * RCAP, 128), fibre_cell.reshape(1, SLOT_DEV), arrived)
    return flow, out


def solution(mesh):
    return jax.shard_map(
        functools.partial(per_device, (mesh.shape["gx"], mesh.shape["gz"])),
        mesh=mesh,
        in_specs=(
            P(None, "gz", "gx", None),
            P(),
            P(None, ("gx", "gz")),
            P(("gx", "gz"), None),
            P(("gx", "gz")),
            P(("gx", "gz"), None),
            P(("gx", "gz")),
        ),
        out_specs=(P(None, "gz", "gx", None), P(None, ("gx", "gz"))),
        check_vma=False,
    )
```

time: 255 us -> 91.1 us (0.36)
  the two profiles are of different devices: /device:TPU:0 before, /device:TPU:25 now
where the time goes in v1:
time: 91.1 us; the launch traced here: 90.9 us
  Pallas kernels  83 us (91%)
  local copies, waits for them, and re-layouts  7.16 us (8%)
    pallas_call x1, Pallas kernels, exchange_call(): pl.pallas_call(functools.partial(exchange_kernel, sizes), out_shape=jax.S...  26.9 us
    pallas_call x1, Pallas kernels, transport_call(): pl.pallas_call(transport_kernel, grid=(3,), out_shape=(jax.ShapeDtypeStru...  22.7 us
    pallas_call x1, Pallas kernels, halo_call(): pl.pallas_call(functools.partial(halo_kernel, sizes), out_shape=(jax.Shap...  22.2 us
    pallas_call x1, Pallas kernels, turn_call(): pl.pallas_call(turn_kernel, out_shape=jax.ShapeDtypeStruct((6, SLOT_DEV),...  11.2 us
    unnamed x18, local copies, waits for them, and re-layouts  7.16 us

profile of v1, /device:TPU:25, one launch (start us, length us, event | category | flops | bytes accessed | tf_op | source)
XLA Modules:
  0.0 90.9 jit_solution(13120866202070773567)
XLA Ops:
  0.6 0.0 copy-start.8
  0.6 0.0 copy-start
  0.7 1.9 %copy-done = f32[3,16,64,256]{3,2,1,0:T(8,128)S(1)} copy-done((f32[3,16,64,256]{3,2,1,0:T(8,128)S(1)}, f32[3,16,64,256]{3,2,1,0:T(8,128)}, u32[]{:S(2)}) %copy-start) | copy-done | bytes 3145752
  2.5 0.0 copy-start.3
  2.5 0.9 copy-done.3
  3.4 0.0 copy-start.5
  3.4 0.7 copy-done.5
  4.2 0.0 copy-start.6
  4.2 0.7 copy-done.6
  4.8 0.0 copy-start.7
  4.8 0.7 copy-done.7
  5.5 22.2 %halo_and_fibres.1 = (f32[3,3,64,256]{3,2,1,0:T(8,128)S(1)}, f32[3,3,64,256]{3,2,1,0:T(8,128)S(1)}, f32[3,16,8,256]{3,2,1,0:T(8,128)S(1)}, f32[3,16,8,256]{3,2,1...) custom-call(f32[3,16,64,256]{3,2,1,0:T(8,128)S(1)} %copy-done, ...), custom_call_target="tpu_custom_call" | custom-call | tf_op jit(solution)/shard_map/halo_and_fibres/pallas_call | solution.py:186
  27.7 0.0 copy-done.8
  27.7 0.0 copy-start.4
  27.7 22.7 %transport_and_rows.1 = (f32[3,16,64,256]{3,2,1,0:T(8,128)}, f32[9,256,128]{2,1,0:T(8,128)S(1)}) custom-call(s32[1,256]{1,0:T(1,128)S(1)} %get-tuple-element.11.slots, f32[3,16,64,256]{3,2,1,0:T(8,128)S(1)} %copy-done, f32[3,3,64,256]{3,2,1,0:T(8,128)S(1)} %get-tuple-element.12.zlo, f32[3,3,64,256]{3,2,1,0:T(8,128)S(1)} %get-tuple-element.13.zhi, ...), custom_call_target="tpu_custom_call" | custom-call | tf_op jit(solution)/shard_map/transport_and_rows/pallas_call | solution.py:269
  50.4 0.0 copy-start.2
  50.4 1.0 %copy-done.2 = f32[9,256,128]{2,1,0:T(8,128)} copy-done((f32[9,256,128]{2,1,0:T(8,128)}, f32[9,256,128]{2,1,0:T(8,128)S(1)}, u32[]{:S(2)}) %copy-start.2) | copy-done | bytes 1179672
  51.4 26.9 %row_exchange.1 = f32[9,128,2,128]{3,2,1,0:T(2,128)} custom-call(f32[9,128,2,128]{3,2,1,0:T(2,128)} %bitcast.8), custom_call_target="tpu_custom_call" | custom-call | tf_op jit(solution)/shard_map/row_exchange/pallas_call | solution.py:331
  78.4 0.0 copy-done.4
  78.4 0.0 copy-start.1
  78.4 1.3 %copy-done.1 = f32[9,128,2,128]{3,2,1,0:T(2,128)S(1)} copy-done((f32[9,128,2,128]{3,2,1,0:T(2,128)S(1)}, f32[9,128,2,128]{3,2,1,0:T(2,128)}, u32[]{:S(2)}) %copy-start.1) | copy-done | bytes 1179672
  79.6 11.2 %gather_and_turn.1 = f32[6,5120]{1,0:T(8,128)} custom-call(f32[9,256,128]{2,1,0:T(8,128)S(1)} %bitcast.7, s32[1,5120]{1,0:T(1,128)S(1)} %bitcast.9, f32[6,5120]{1,0:T(8,128)S(1)} %get-tuple-element.19.arrived), custom_call_target="tpu_custom_call" | custom-call | tf_op jit(solution)/shard_map/gather_and_turn/pallas_call | solution.py:380
Async XLA Ops:
  0.6 27.1 %copy-start.8 = (f32[256]{0:T(256)S(1)}, f32[256]{0:T(256)}, u32[]{:S(2)}) copy-start(f32[256]{0:T(256)} %param.8) | copy-start | bytes 3076
  0.6 1.9 %copy-start = (f32[3,16,64,256]{3,2,1,0:T(8,128)S(1)}, f32[3,16,64,256]{3,2,1,0:T(8,128)}, u32[]{:S(2)}) copy-start(f32[3,16,64,256]{3,2,1,0:T(8,128)} %velocity.3) | copy-start | bytes 9437188
  2.5 0.9 copy-start.3
  3.4 0.7 copy-start.5
  4.2 0.7 copy-start.6
  4.8 0.7 copy-start.7
  27.7 50.7 %copy-start.4 = (s32[5120]{0:T(1024)S(1)}, s32[5120]{0:T(1024)}, u32[]{:S(2)}) copy-start(s32[5120]{0:T(1024)} %param.13) | copy-start | bytes 61444
  50.4 1.0 %copy-start.2 = (f32[9,256,128]{2,1,0:T(8,128)}, f32[9,256,128]{2,1,0:T(8,128)S(1)}, u32[]{:S(2)}) copy-start(f32[9,256,128]{2,1,0:T(8,128)S(1)} %get-tuple-element.18) | copy-start | bytes 3538948
  78.4 1.3 %copy-start.1 = (f32[9,128,2,128]{3,2,1,0:T(2,128)S(1)}, f32[9,128,2,128]{3,2,1,0:T(2,128)}, u32[]{:S(2)}) copy-start(f32[9,128,2,128]{3,2,1,0:T(2,128)} %row_exchange.1) | copy-start | bytes 3538948

commit v2 on v1

v2 whole, which is shorter than its diff:
```python
import functools

import jax
import jax.numpy as jnp
from jax import lax
from jax.experimental import pallas as pl
from jax.experimental.pallas import tpu as pltpu
from jax.sharding import PartitionSpec as P

FIB_DEV = 4096
CAP = 128
SLOT_DEV = 5120
RCAP = 2
CX, CZ, NY = 64, 16, 256
XW = 72
ROWS = 2048

DIFFUSION = 0.1
ADVECTION = 0.4
SHAPE_FACTOR = 0.9
TURN_STEP = 0.25

MESH = pl.DeviceIdType.MESH
F32 = jnp.float32
BF16 = jnp.bfloat16
I32 = jnp.int32
MIB = 2**20


def code_offset(code):
    return code * CAP if code <= 4 else FIB_DEV + (code - 1) * CAP


def place(device, gz_size):
    return (device // gz_size, lax.rem(device, gz_size))


def split3(x):
    hi = x.astype(BF16).astype(F32)
    mid = (x - hi).astype(BF16).astype(F32)
    return hi, mid, x - hi - mid


def iota(shape, dim):
    return lax.broadcasted_iota(I32, shape, dim)


def slot_list(rows_ref, readers_ref):
    n = rows_ref.shape[1]
    rows, readers = rows_ref[...], readers_ref[...]
    sub, lane = iota((n, n), 0), iota((n, n), 1)
    diag = sub == lane

    def column(row):
        return jnp.sum(jnp.where(diag, jnp.broadcast_to(row, (n, n)), 0), axis=1, keepdims=True)

    same = (column(readers) == readers) & (sub < lane)
    rank = jnp.sum(same.astype(I32), axis=0, keepdims=True)
    slot = column(readers * RCAP + rank)
    table_row = column(((rows // 128) * 2 + rows % 2) * CX + (rows // 2) % CX)
    slots = iota((n, 256), 1)
    return jnp.sum(jnp.where(slot == slots, table_row - ROWS, 0), axis=0, keepdims=True) + ROWS


def fibre_ranks(code):
    masks = [code == c for c in range(9)]
    ones = jnp.concatenate([m.astype(F32) for m in masks], axis=0).astype(BF16)
    tri = (iota((128, 128), 0) < iota((128, 128), 1)).astype(BF16)
    before = jnp.dot(ones, tri, preferred_element_type=F32)
    total = jnp.dot(ones, jnp.ones((128, 128), BF16), preferred_element_type=F32)
    low = (iota((32, 32), 1) < iota((32, 32), 0)).astype(BF16)
    rank = jnp.zeros((32, 128), F32)
    for c in range(9):
        part = total[32 * c : 32 * c + 32]
        above = jnp.dot(low, part.astype(BF16), preferred_element_type=F32)
        rank = jnp.where(masks[c], before[32 * c : 32 * c + 32] + above, rank)
        if c == 4:
            stay = jnp.sum(part, axis=0, keepdims=True)[:, 0:1]
    return rank.astype(I32), stay.astype(I32)


def as_row(x):
    return jnp.concatenate([x[r : r + 1] for r in range(x.shape[0])], axis=1)


def compact(records, shift, stay):
    shape = records.shape
    n = shape[1]
    for b in range(11):
        w = 1 << b
        came_shift = pltpu.roll(shift, n - w, 1)
        came = pltpu.roll(records, n - w, 1)
        arrive = (came_shift & w) != 0
        leave = (shift & w) != 0
        records = jnp.where(arrive, came, records)
        shift = jnp.where(arrive, came_shift, jnp.where(leave, 0, shift))
    return jnp.where(iota(shape, 1) < stay, records, 0.0)


def pack_fibres(fibres_ref, code_ref, split_ref, pieces_ref, arrived_ref):
    code = code_ref[...]
    rank, stay = fibre_ranks(code)
    fibre = iota((32, 128), 0) * 128 + iota((32, 128), 1)
    shift = as_row(jnp.where(code == 4, fibre - rank, 0))
    slot = as_row(jnp.where(code == 4, -1, jnp.where(code < 4, code, code - 1) * CAP + rank))
    split_ref[...] = jnp.zeros(split_ref.shape, F32)
    for i, part in enumerate(split3(fibres_ref[...])):
        split_ref[8 * i : 8 * i + 6, :] = part
    acc = jnp.zeros((24, 8 * CAP), F32)
    step = 512
    for k in range(FIB_DEV // step):
        onehot = (iota((8 * CAP, step), 0) == slot[:, k * step : k * step + step]).astype(F32).astype(BF16)
        acc = acc + lax.dot_general(
            split_ref[:, k * step : k * step + step].astype(BF16),
            onehot,
            (((1,), (1,)), ((), ())),
            preferred_element_type=F32,
        )
    packed = acc[0:6] + acc[8:14] + acc[16:22]
    for j in range(8):
        pieces_ref[j] = packed[:, j * CAP : j * CAP + CAP]
    records = fibres_ref[...]
    arrived_ref[:, 4 * CAP : 4 * CAP + FIB_DEV] = compact(records, jnp.broadcast_to(shift, records.shape), stay)


def advance(old, new, count, ahead, behind, unroll):
    @pl.loop(0, count, unroll=unroll)
    def _(z):
        centre = old[z + 1]
        xp, xm, yp, ym = beside(centre)
        near = (old[z] + old[z + 2]) + (yp + ym)
        new[z] = (1.0 - 6.0 * DIFFUSION) * centre + DIFFUSION * near + (ahead * xp + behind * xm)


def beside(plane):
    lane = iota(plane.shape, 1)
    xp = pltpu.roll(plane, XW - 1, 0)
    xm = pltpu.roll(plane, 1, 0)
    yp = jnp.where(lane == NY - 1, 0.0, pltpu.roll(plane, NY - 1, 1))
    ym = jnp.where(lane == 0, 0.0, pltpu.roll(plane, 1, 1))
    return xp, xm, yp, ym


def flow_kernel(
    sizes, velocity, flow_hbm, fibres_hbm, code_hbm, rows_hbm, readers_hbm,
    out, recv_out, arrived_out,
    first, second, third, grads, send, recv, side, corner,
    flow, fibres, code, rows, readers, split, pieces, arrived, slots, slots_smem,
    load_sem, small_sem, slot_sem, out_sem, halo_send, halo_recv, fib_send, fib_recv,
    row_send, row_recv, row_own, last_sem,
):
    nx, nz = sizes
    count = nx * nz
    ix, iz = lax.axis_index("gx"), lax.axis_index("gz")
    me = ix * nz + iz

    def at(dx, dz):
        return (lax.rem(ix + dx + nx, nx), lax.rem(iz + dz + nz, nz))

    barrier = pltpu.get_barrier_semaphore()

    @pl.loop(1, count)
    def _(i):
        there = place(lax.rem(me + i, count), nz)
        pl.semaphore_signal(barrier, inc=1, device_id=there, device_id_type=MESH)

    small = [
        pltpu.make_async_copy(src, dst, small_sem.at[i])
        for i, (src, dst) in enumerate(
            ((rows_hbm, rows), (readers_hbm, readers), (code_hbm, code), (fibres_hbm, fibres), (flow_hbm, flow))
        )
    ]
    for copy in small:
        copy.start()
    loads = [
        pltpu.make_async_copy(velocity.at[c], first.at[c, 3:19, 0:64], load_sem.at[c]) for c in range(3)
    ]
    for copy in loads:
        copy.start()
    pl.semaphore_wait(barrier, count - 1)

    halos = []
    for c in range(3):
        part = []
        for i, (src, dst, dx, dz) in enumerate((
            (velocity.at[c, 13:16], first.at[c, 0:3, 0:64], 0, 1),
            (velocity.at[c, 0:3], first.at[c, 19:22, 0:64], 0, -1),
            (velocity.at[c, :, 56:64], side.at[c, 0], 1, 0),
            (velocity.at[c, :, 0:8], side.at[c, 1], -1, 0),
            (velocity.at[c, 14:16, 56:64], corner.at[c, 0], 1, 1),
            (velocity.at[c, 14:16, 0:8], corner.at[c, 1], -1, 1),
            (velocity.at[c, 0:2, 56:64], corner.at[c, 2], 1, -1),
            (velocity.at[c, 0:2, 0:8], corner.at[c, 3], -1, -1),
        )):
            copy = pltpu.make_async_remote_copy(
                src, dst, halo_send.at[8 * c + i], halo_recv.at[8 * c + i], device_id=at(dx, dz), device_id_type=MESH
            )
            copy.start()
            part.append(copy)
        halos.append(part)

    small[0].wait()
    small[1].wait()
    slots[...] = slot_list(rows, readers)
    to_scalars = pltpu.make_async_copy(slots, slots_smem, slot_sem)
    to_scalars.start()
    small[2].wait()
    small[3].wait()
    pack_fibres(fibres, code, split, pieces, arrived)
    moved = []
    around = [(dx, dz) for dx in (-1, 0, 1) for dz in (-1, 0, 1) if (dx, dz) != (0, 0)]
    for j, (dx, dz) in enumerate(around):
        off = code_offset((dx + 1) * 3 + dz + 1)
        copy = pltpu.make_async_remote_copy(
            pieces.at[j], arrived.at[:, off : off + CAP], fib_send.at[j], fib_recv.at[j],
            device_id=at(dx, dz), device_id_type=MESH,
        )
        copy.start()
        moved.append(copy)
    small[4].wait()
    to_scalars.wait()

    ahead = DIFFUSION - 0.5 * ADVECTION * flow[...]
    behind = DIFFUSION + 0.5 * ADVECTION * flow[...]
    sub = iota((1, 8, NY), 1) < 4
    grads[:, ROWS : ROWS + 8, :] = jnp.zeros((3, 8, 128), F32)
    outs, owns = [], []
    for c in range(3):
        loads[c].wait()
        for copy in halos[c]:
            copy.wait_recv()
        here, done = first.at[c], third.at[c]
        here[3:19, 64:72, :] = jnp.where(sub, side[c, 1], side[c, 0])
        here[1:3, 64:72, :] = jnp.where(sub, corner[c, 1], corner[c, 0])
        here[19:21, 64:72, :] = jnp.where(sub, corner[c, 3], corner[c, 2])
        advance(here, second, 20, ahead, behind, 5)
        advance(second, done, 18, ahead, behind, 6)
        copy = pltpu.make_async_copy(done.at[1:17, 0:64], out.at[c], out_sem.at[c])
        copy.start()
        outs.append(copy)

        @pl.loop(0, CZ, unroll=4)
        def _(z):
            xp, xm, yp, ym = beside(done[z + 1])
            along_z = done[z + 2] - done[z]
            for j, d in enumerate((xp - xm, yp - ym, along_z)):
                d = 0.5 * d
                for h in range(2):
                    base = pl.multiple_of((z * 2 + h) * CX, CX)
                    grads[j, pl.ds(base, CX), :] = d[0:64, h * 128 : h * 128 + 128]

        @pl.loop(0, count, unroll=4)
        def _(t):
            for k in range(RCAP):
                row = slots_smem[0, RCAP * t + k]
                for j in range(3):
                    send[c, t, 3 * k + j : 3 * k + j + 1, :] = grads[j, pl.ds(row, 1), :]

        own = pltpu.make_async_copy(send.at[c, me, 0:6], recv.at[c, me, 0:6], row_own.at[c])
        own.start()
        owns.append(own)

        @pl.loop(1, count)
        def _(i):
            reader = lax.rem(me + i, count)
            pltpu.make_async_remote_copy(
                send.at[c, reader, 0:6], recv.at[c, me, 0:6], row_send.at[c], row_recv.at[c],
                device_id=place(reader, nz), device_id_type=MESH,
            ).start()

    for copy in moved:
        copy.wait()
    last = [pltpu.make_async_copy(arrived, arrived_out, last_sem.at[3])]
    last[0].start()
    for c in range(3):
        every = pl.ds(0, count - 1)
        pltpu.make_async_copy(recv.at[c, every, 0:6], recv.at[c, every, 0:6], row_recv.at[c]).wait()
        owns[c].wait()
        copy = pltpu.make_async_copy(recv.at[c], recv_out.at[c], last_sem.at[c])
        copy.start()
        last.append(copy)
    for c in range(3):
        every = pl.ds(0, count - 1)
        pltpu.make_async_copy(send.at[c, every, 0:6], send.at[c, every, 0:6], row_send.at[c]).wait()
        outs[c].wait()
        for copy in halos[c]:
            copy.wait_send()
    for copy in last:
        copy.wait()


def hbm_spec():
    return pl.BlockSpec(memory_space=pltpu.HBM)


def any_spec():
    return pl.BlockSpec(memory_space=pl.ANY)


def vmem_spec():
    return pl.BlockSpec(memory_space=pltpu.VMEM)


def flow_call(sizes, *operands):
    count = sizes[0] * sizes[1]
    dma = pltpu.SemaphoreType.DMA
    return pl.pallas_call(
        functools.partial(flow_kernel, sizes),
        out_shape=(
            jax.ShapeDtypeStruct((3, CZ, CX, NY), F32),
            jax.ShapeDtypeStruct((3, count, 8, 128), F32),
            jax.ShapeDtypeStruct((6, SLOT_DEV), F32),
        ),
        in_specs=[hbm_spec()] * 6,
        out_specs=(hbm_spec(),) * 3,
        scratch_shapes=[
            pltpu.VMEM((3, 22, XW, NY), F32),
            pltpu.VMEM((20, XW, NY), F32),
            pltpu.VMEM((3, 18, XW, NY), F32),
            pltpu.VMEM((3, ROWS + 8, 128), F32),
            pltpu.VMEM((3, count, 8, 128), F32),
            pltpu.VMEM((3, count, 8, 128), F32),
            pltpu.VMEM((3, 2, CZ, 8, NY), F32),
            pltpu.VMEM((3, 4, 2, 8, NY), F32),
            pltpu.VMEM((1, NY), F32),
            pltpu.VMEM((6, FIB_DEV), F32),
            pltpu.VMEM((32, 128), I32),
            pltpu.VMEM((1, 192), I32),
            pltpu.VMEM((1, 192), I32),
            pltpu.VMEM((24, FIB_DEV), F32),
            pltpu.VMEM((8, 6, CAP), F32),
            pltpu.VMEM((6, SLOT_DEV), F32),
            pltpu.VMEM((1, 256), I32),
            pltpu.SMEM((1, 256), I32),
            dma((3,)), dma((5,)), dma, dma((3,)), dma((24,)), dma((24,)), dma((8,)), dma((8,)),
            dma((3,)), dma((3,)), dma((3,)), dma((4,)),
        ],
        compiler_params=pltpu.CompilerParams(
            collective_id=0, has_side_effects=True, vmem_limit_bytes=60 * MIB
        ),
        name="flow_and_rows",
    )(*operands)


def jeffery(orient, tensor):
    along = [sum(tensor[3 * i + j] * orient[j] for j in range(3)) for i in range(3)]
    across = [sum(tensor[3 * j + i] * orient[j] for j in range(3)) for i in range(3)]
    stretch = sum(orient[i] * along[i] for i in range(3))
    turned = []
    for i in range(3):
        strain = 0.5 * (along[i] + across[i])
        rotation = 0.5 * (along[i] - across[i])
        turned.append(orient[i] + TURN_STEP * (rotation + SHAPE_FACTOR * (strain - stretch * orient[i])))
    return turned


def turn_kernel(recv, cell, arrived, flow, out, flow_out, table, flow_sem):
    copy = pltpu.make_async_copy(flow, flow_out, flow_sem)
    copy.start()
    count = recv.shape[1]
    for c in range(3):
        rows = recv.at[c].reshape(count * 8, 128)
        for j in range(3):
            q = 3 * c + j
            for k in range(RCAP):
                block = jnp.transpose(rows[pl.ds(3 * k + j, count, 8), :])
                hi = block.astype(BF16)
                table[128 * q : 128 * q + 128, count * k : count * (k + 1)] = hi
                table[128 * q : 128 * q + 128, 256 + count * k : 256 + count * (k + 1)] = (
                    block - hi.astype(F32)
                ).astype(BF16)
    width = 256

    @pl.loop(0, SLOT_DEV // width)
    def _(n):
        base = pl.multiple_of(n * width, width)
        here = cell[:, pl.ds(base, width)]
        row = here // 128
        row = (row % RCAP) * count + row // RCAP
        onehot = (iota((256, width), 0) == row).astype(F32).astype(BF16)
        picked = jnp.dot(table[...], jnp.concatenate([onehot, onehot], axis=0), preferred_element_type=F32)
        lane = iota((128, width), 0) == here % 128
        tensor = [
            jnp.sum(jnp.where(lane, picked[128 * q : 128 * q + 128], 0.0), axis=0, keepdims=True) for q in range(9)
        ]
        records = arrived[:, pl.ds(base, width)]
        turned = jeffery([records[3 + i : 4 + i] for i in range(3)], tensor)
        out[0:3, pl.ds(base, width)] = records[0:3]
        for i in range(3):
            out[3 + i : 4 + i, pl.ds(base, width)] = turned[i]

    copy.wait()


def turn_call(recv, cell, arrived, flow):
    return pl.pallas_call(
        turn_kernel,
        out_shape=(jax.ShapeDtypeStruct((6, SLOT_DEV), F32), jax.ShapeDtypeStruct(flow.shape, F32)),
        in_specs=[vmem_spec()] * 3 + [any_spec()],
        out_specs=(vmem_spec(), hbm_spec()),
        scratch_shapes=[pltpu.VMEM((1152, 512), BF16), pltpu.SemaphoreType.DMA],
        compiler_params=pltpu.CompilerParams(vmem_limit_bytes=60 * MIB),
        name="gather_and_turn",
    )(recv, cell, arrived, flow)


def per_device(sizes, velocity, mean_flow, fibres, moves, grad_rows, grad_readers, fibre_cell):
    flow, recv, arrived = flow_call(
        sizes, velocity, mean_flow.reshape(1, NY), fibres, moves.reshape(32, 128),
        grad_rows.reshape(1, -1), grad_readers.reshape(1, -1),
    )
    out, flow = turn_call(recv, fibre_cell.reshape(1, SLOT_DEV), arrived, flow)
    return flow, out


def solution(mesh):
    return jax.shard_map(
        functools.partial(per_device, (mesh.shape["gx"], mesh.shape["gz"])),
        mesh=mesh,
        in_specs=(
            P(None, "gz", "gx", None),
            P(),
            P(None, ("gx", "gz")),
            P(("gx", "gz"), None),
            P(("gx", "gz")),
            P(("gx", "gz"), None),
            P(("gx", "gz")),
        ),
        out_specs=(P(None, "gz", "gx", None), P(None, ("gx", "gz"))),
        check_vma=False,
    )
```

time: 91.1 us -> 147 us (1.61)
  the two profiles are of different devices: /device:TPU:25 before, /device:TPU:0 now
where the time goes in v2:
time: 147 us; the launch traced here: 146 us
  Pallas kernels  145 us (99%)
    pallas_call x1, Pallas kernels, turn_call(): pl.pallas_call(turn_kernel, out_shape=(jax.ShapeDtypeStruct((6, SLOT_DEV)...  98.5 us
    pallas_call x1, Pallas kernels, flow_call(): pl.pallas_call(functools.partial(flow_kernel, sizes), out_shape=(jax.Shap...  46.5 us

profile of v2, /device:TPU:0, one launch (start us, length us, event | category | flops | bytes accessed | tf_op | source)
XLA Modules:
  0.0 145.6 jit_solution(13266829202638927675)
XLA Ops:
  0.6 46.5 %flow_and_rows.1 = (f32[3,16,64,256]{3,2,1,0:T(8,128)}, f32[3,128,8,128]{3,2,1,0:T(8,128)}, f32[6,5120]{1,0:T(8,128)}) custom-call(f32[3,16,64,256]{3,2,1,0:T(8,128)} %velocity.1, f32[1,256]{1,0:T(1,128)} %bitcast.7, f32[6,4096]{1,0:T(8,128)} %fibres_hbm.1, s32[32,128]{1,0:T(8,128)} %bitcast.6, s32[1,192]{1,0:T(1,128)} %bitcast.8, s32[1,192]{1,0:T(1,128)} %bitcast.9), custom_call_target="tpu_custom_call" | custom-call | tf_op jit(solution)/shard_map/flow_and_rows/pallas_call | solution.py:307
  47.1 98.5 %gather_and_turn.1 = (f32[6,5120]{1,0:T(8,128)}, f32[3,16,64,256]{3,2,1,0:T(8,128)}) custom-call(f32[3,128,8,128]{3,2,1,0:T(8,128)} %get-tuple-element.7.recv, s32[1,5120]{1,0:T(1,128)} %bitcast.5, f32[6,5120]{1,0:T(8,128)} %get-tuple-element.8.arrived, f32[3,16,64,256]{3,2,1,0:T(8,128)} %get-tuple-element.9.flow), custom_call_target="tpu_custom_call" | custom-call | tf_op jit(solution)/shard_map/gather_and_turn/pallas_call | solution.py:396

commit v3 on v2

--- a/solution.py
+++ b/solution.py
@@ -142,12 +142,13 @@
 
 
 def flow_kernel(
-    sizes, velocity, flow_hbm, fibres_hbm, code_hbm, rows_hbm, readers_hbm,
-    out, recv_out, arrived_out,
-    first, second, third, grads, send, recv, side, corner,
-    flow, fibres, code, rows, readers, split, pieces, arrived, slots, slots_smem,
+    sizes, velocity, flow_hbm, fibres_hbm, code_hbm, rows_hbm, readers_hbm, cell_hbm,
+    out, recv_out, tensor_out, arrived_out,
+    first, second, third, grads, send, recv, side, edge, corner,
+    flow, fibres, code, rows, readers, cell, split, pieces, arrived, slots, slots_smem,
+    onehot, table, tensor,
     load_sem, small_sem, slot_sem, out_sem, halo_send, halo_recv, fib_send, fib_recv,
-    row_send, row_recv, row_own, last_sem,
+    corner_send, corner_recv, row_send, row_recv, row_own, last_sem, known,
 ):
     nx, nz = sizes
     count = nx * nz
@@ -157,82 +158,113 @@
     def at(dx, dz):
         return (lax.rem(ix + dx + nx, nx), lax.rem(iz + dz + nz, nz))
 
+    around = [(dx, dz) for dx in (-1, 0, 1) for dz in (-1, 0, 1) if (dx, dz) != (0, 0)]
+
+    def greet(semaphore, reach):
+        there = {((dx * reach) % nx, (dz * reach) % nz) for dx, dz in around} - {(0, 0)}
+        for dx, dz in sorted(there):
+            pl.semaphore_signal(semaphore, inc=1, device_id=at(dx, dz), device_id_type=MESH)
+        return len(there)
+
     barrier = pltpu.get_barrier_semaphore()
-
-    @pl.loop(1, count)
-    def _(i):
-        there = place(lax.rem(me + i, count), nz)
-        pl.semaphore_signal(barrier, inc=1, device_id=there, device_id_type=MESH)
-
-    small = [
-        pltpu.make_async_copy(src, dst, small_sem.at[i])
-        for i, (src, dst) in enumerate(
-            ((rows_hbm, rows), (readers_hbm, readers), (code_hbm, code), (fibres_hbm, fibres), (flow_hbm, flow))
-        )
-    ]
-    for copy in small:
-        copy.start()
+    greeted = greet(barrier, 1)
+
     loads = [
         pltpu.make_async_copy(velocity.at[c], first.at[c, 3:19, 0:64], load_sem.at[c]) for c in range(3)
     ]
-    for copy in loads:
+    small = [
+        pltpu.make_async_copy(src, dst, small_sem.at[i])
+        for i, (src, dst) in enumerate((
+            (rows_hbm, rows), (readers_hbm, readers), (code_hbm, code), (fibres_hbm, fibres), (flow_hbm, flow),
+            (cell_hbm, cell),
+        ))
+    ]
+    for copy in small + loads:
         copy.start()
-    pl.semaphore_wait(barrier, count - 1)
-
-    halos = []
-    for c in range(3):
-        part = []
-        for i, (src, dst, dx, dz) in enumerate((
+    pl.semaphore_wait(barrier, greeted)
+
+    def remote(src, dst, send_sem, recv_sem, dx, dz):
+        copy = pltpu.make_async_remote_copy(
+            src, dst, send_sem, recv_sem, device_id=at(dx, dz), device_id_type=MESH
+        )
+        copy.start()
+        return copy
+
+    def send_halo(c):
+        faces = (
             (velocity.at[c, 13:16], first.at[c, 0:3, 0:64], 0, 1),
             (velocity.at[c, 0:3], first.at[c, 19:22, 0:64], 0, -1),
             (velocity.at[c, :, 56:64], side.at[c, 0], 1, 0),
             (velocity.at[c, :, 0:8], side.at[c, 1], -1, 0),
-            (velocity.at[c, 14:16, 56:64], corner.at[c, 0], 1, 1),
-            (velocity.at[c, 14:16, 0:8], corner.at[c, 1], -1, 1),
-            (velocity.at[c, 0:2, 56:64], corner.at[c, 2], 1, -1),
-            (velocity.at[c, 0:2, 0:8], corner.at[c, 3], -1, -1),
-        )):
-            copy = pltpu.make_async_remote_copy(
-                src, dst, halo_send.at[8 * c + i], halo_recv.at[8 * c + i], device_id=at(dx, dz), device_id_type=MESH
-            )
-            copy.start()
-            part.append(copy)
-        halos.append(part)
-
+        )
+        return [
+            remote(src, dst, halo_send.at[4 * c + i], halo_recv.at[4 * c + i], dx, dz)
+            for i, (src, dst, dx, dz) in enumerate(faces)
+        ]
+
+    halos = [send_halo(0)]
     small[0].wait()
     small[1].wait()
     slots[...] = slot_list(rows, readers)
     to_scalars = pltpu.make_async_copy(slots, slots_smem, slot_sem)
     to_scalars.start()
+    greeted = greet(known.at[0], 1)
+
+    for copy in loads:
+        copy.wait()
+    diagonal = [(1, 1), (-1, 1), (1, -1), (-1, -1)]
+    corners = []
+    for i, (dx, dz) in enumerate(diagonal):
+        near, far = (18, 17) if dz == 1 else (3, 4)
+        x1, x2 = (63, 62) if dx == 1 else (0, 1)
+        for c in range(3):
+            for r, (z, x) in enumerate(((near, x1), (near, x2), (far, x1))):
+                edge[i, 3 * c + r] = first[c, z, x : x + 1, :]
+        corners.append(remote(edge.at[i], corner.at[i], corner_send.at[i], corner_recv.at[i], dx, dz))
+
+    pl.semaphore_wait(known.at[0], greeted)
+    greeted = greet(known.at[1], 2)
     small[2].wait()
     small[3].wait()
     pack_fibres(fibres, code, split, pieces, arrived)
     moved = []
-    around = [(dx, dz) for dx in (-1, 0, 1) for dz in (-1, 0, 1) if (dx, dz) != (0, 0)]
     for j, (dx, dz) in enumerate(around):
         off = code_offset((dx + 1) * 3 + dz + 1)
-        copy = pltpu.make_async_remote_copy(
-            pieces.at[j], arrived.at[:, off : off + CAP], fib_send.at[j], fib_recv.at[j],
-            device_id=at(dx, dz), device_id_type=MESH,
+        moved.append(
+            remote(pieces.at[j], arrived.at[:, off : off + CAP], fib_send.at[j], fib_recv.at[j], dx, dz)
         )
-        copy.start()
-        moved.append(copy)
+    halos.append(send_halo(1))
+    pl.semaphore_wait(known.at[1], greeted)
+    greeted = greet(known.at[2], 4)
+    small[5].wait()
+    width = 512
+
+    @pl.loop(0, SLOT_DEV // width)
+    def _(n):
+        base = pl.multiple_of(n * width, width)
+        onehot[:, pl.ds(base, width)] = row_onehot(cell[:, pl.ds(base, width)], count)
+
     small[4].wait()
     to_scalars.wait()
-
     ahead = DIFFUSION - 0.5 * ADVECTION * flow[...]
     behind = DIFFUSION + 0.5 * ADVECTION * flow[...]
     sub = iota((1, 8, NY), 1) < 4
     grads[:, ROWS : ROWS + 8, :] = jnp.zeros((3, 8, 128), F32)
     outs, owns = [], []
     for c in range(3):
-        loads[c].wait()
         for copy in halos[c]:
             copy.wait_recv()
+        if c == 0:
+            halos.append(send_halo(2))
+            for copy in corners:
+                copy.wait_recv()
         here, done = first.at[c], third.at[c]
         here[3:19, 64:72, :] = jnp.where(sub, side[c, 1], side[c, 0])
-        here[1:3, 64:72, :] = jnp.where(sub, corner[c, 1], corner[c, 0])
-        here[19:21, 64:72, :] = jnp.where(sub, corner[c, 3], corner[c, 2])
+        for i, (dx, dz) in enumerate(diagonal):
+            near, far = (2, 1) if dz == 1 else (19, 20)
+            x1, x2 = (71, 70) if dx == 1 else (64, 65)
+            for r, (z, x) in enumerate(((near, x1), (near, x2), (far, x1))):
+                here[z, x : x + 1, :] = corner[i, 3 * c + r]
         advance(here, second, 20, ahead, behind, 5)
         advance(second, done, 18, ahead, behind, 6)
         copy = pltpu.make_async_copy(done.at[1:17, 0:64], out.at[c], out_sem.at[c])
@@ -256,6 +288,8 @@
                 for j in range(3):
                     send[c, t, 3 * k + j : 3 * k + j + 1, :] = grads[j, pl.ds(row, 1), :]
 
+        if c == 0:
+            pl.semaphore_wait(known.at[2], greeted)
         own = pltpu.make_async_copy(send.at[c, me, 0:6], recv.at[c, me, 0:6], row_own.at[c])
         own.start()
         owns.append(own)
@@ -270,23 +304,60 @@
 
     for copy in moved:
         copy.wait()
-    last = [pltpu.make_async_copy(arrived, arrived_out, last_sem.at[3])]
+    last = [pltpu.make_async_copy(arrived, arrived_out, last_sem.at[0])]
     last[0].start()
+    every = pl.ds(0, count - 1)
     for c in range(3):
-        every = pl.ds(0, count - 1)
         pltpu.make_async_copy(recv.at[c, every, 0:6], recv.at[c, every, 0:6], row_recv.at[c]).wait()
         owns[c].wait()
-        copy = pltpu.make_async_copy(recv.at[c], recv_out.at[c], last_sem.at[c])
-        copy.start()
-        last.append(copy)
+        if c < 2:
+            fill_table(recv.at[c], table)
+            width = 1024
+
+            @pl.loop(0, SLOT_DEV // width)
+            def _(n):
+                part = pl.ds(pl.multiple_of(n * width, width), width)
+                for j, row in enumerate(pick(table, onehot[:, part], cell[:, part])):
+                    tensor[3 * c + j : 3 * c + j + 1, part] = row
+
+    last.append(pltpu.make_async_copy(recv.at[2], recv_out, last_sem.at[1]))
+    last.append(pltpu.make_async_copy(tensor, tensor_out, last_sem.at[2]))
+    last[1].start()
+    last[2].start()
     for c in range(3):
-        every = pl.ds(0, count - 1)
         pltpu.make_async_copy(send.at[c, every, 0:6], send.at[c, every, 0:6], row_send.at[c]).wait()
         outs[c].wait()
         for copy in halos[c]:
             copy.wait_send()
+    for copy in corners:
+        copy.wait_send()
     for copy in last:
         copy.wait()
+
+
+def row_onehot(cell, count):
+    row = cell // 128
+    row = (row % RCAP) * count + row // RCAP
+    return (iota((RCAP * count, cell.shape[1]), 0) == row).astype(F32).astype(BF16)
+
+
+def fill_table(recv, table):
+    count = recv.shape[0]
+    flat = recv.reshape(count * 8, 128)
+    for j in range(3):
+        for k in range(RCAP):
+            block = jnp.transpose(flat[pl.ds(3 * k + j, count, 8), :])
+            hi = block.astype(BF16)
+            at = count * k
+            table[128 * j : 128 * j + 128, at : at + count] = hi
+            at = at + RCAP * count
+            table[128 * j : 128 * j + 128, at : at + count] = (block - hi.astype(F32)).astype(BF16)
+
+
+def pick(table, onehot, cell):
+    rows = jnp.dot(table[...], jnp.concatenate([onehot, onehot], axis=0), preferred_element_type=F32)
+    lane = iota((128, cell.shape[1]), 0) == cell % 128
+    return [jnp.sum(jnp.where(lane, rows[128 * j : 128 * j + 128], 0.0), axis=0, keepdims=True) for j in range(3)]
 
 
 def hbm_spec():
@@ -308,11 +379,12 @@
         functools.partial(flow_kernel, sizes),
         out_shape=(
             jax.ShapeDtypeStruct((3, CZ, CX, NY), F32),
-            jax.ShapeDtypeStruct((3, count, 8, 128), F32),
+            jax.ShapeDtypeStruct((count, 8, 128), F32),
+            jax.ShapeDtypeStruct((6, SLOT_DEV), F32),
             jax.ShapeDtypeStruct((6, SLOT_DEV), F32),
         ),
-        in_specs=[hbm_spec()] * 6,
-        out_specs=(hbm_spec(),) * 3,
+        in_specs=[hbm_spec()] * 7,
+        out_specs=(hbm_spec(),) * 4,
         scratch_shapes=[
             pltpu.VMEM((3, 22, XW, NY), F32),
             pltpu.VMEM((20, XW, NY), F32),
@@ -321,19 +393,24 @@
             pltpu.VMEM((3, count, 8, 128), F32),
             pltpu.VMEM((3, count, 8, 128), F32),
             pltpu.VMEM((3, 2, CZ, 8, NY), F32),
-            pltpu.VMEM((3, 4, 2, 8, NY), F32),
+            pltpu.VMEM((4, 9, 1, NY), F32),
+            pltpu.VMEM((4, 9, 1, NY), F32),
             pltpu.VMEM((1, NY), F32),
             pltpu.VMEM((6, FIB_DEV), F32),
             pltpu.VMEM((32, 128), I32),
             pltpu.VMEM((1, 192), I32),
             pltpu.VMEM((1, 192), I32),
+            pltpu.VMEM((1, SLOT_DEV), I32),
             pltpu.VMEM((24, FIB_DEV), F32),
             pltpu.VMEM((8, 6, CAP), F32),
             pltpu.VMEM((6, SLOT_DEV), F32),
             pltpu.VMEM((1, 256), I32),
             pltpu.SMEM((1, 256), I32),
-            dma((3,)), dma((5,)), dma, dma((3,)), dma((24,)), dma((24,)), dma((8,)), dma((8,)),
-            dma((3,)), dma((3,)), dma((3,)), dma((4,)),
+            pltpu.VMEM((RCAP * count, SLOT_DEV), BF16),
+            pltpu.VMEM((384, 2 * RCAP * count), BF16),
+            pltpu.VMEM((6, SLOT_DEV), F32),
+            dma((3,)), dma((6,)), dma, dma((3,)), dma((12,)), dma((12,)), dma((8,)), dma((8,)),
+            dma((4,)), dma((4,)), dma((3,)), dma((3,)), dma((3,)), dma((3,)), pltpu.SemaphoreType.REGULAR((3,)),
         ],
         compiler_params=pltpu.CompilerParams(
             collective_id=0, has_side_effects=True, vmem_limit_bytes=60 * MIB
@@ -354,62 +431,59 @@
     return turned
 
 
-def turn_kernel(recv, cell, arrived, flow, out, flow_out, table, flow_sem):
-    copy = pltpu.make_async_copy(flow, flow_out, flow_sem)
-    copy.start()
-    count = recv.shape[1]
-    for c in range(3):
-        rows = recv.at[c].reshape(count * 8, 128)
-        for j in range(3):
-            q = 3 * c + j
-            for k in range(RCAP):
-                block = jnp.transpose(rows[pl.ds(3 * k + j, count, 8), :])
-                hi = block.astype(BF16)
-                table[128 * q : 128 * q + 128, count * k : count * (k + 1)] = hi
-                table[128 * q : 128 * q + 128, 256 + count * k : 256 + count * (k + 1)] = (
-                    block - hi.astype(F32)
-                ).astype(BF16)
-    width = 256
-
-    @pl.loop(0, SLOT_DEV // width)
+def turn_kernel(recv, tensor, cell, arrived, flow, out, flow_out, table, held, in_sem, out_sem):
+    bring = pltpu.make_async_copy(flow, held, in_sem)
+    bring.start()
+    store = pltpu.make_async_copy(held, flow_out, out_sem)
+    count = recv.shape[0]
+    fill_table(recv, table)
+    width = 1024
+
+    def turn(n):
+        part = pl.ds(pl.multiple_of(n * width, width), width)
+        here = cell[:, part]
+        rows = [tensor[i : i + 1, part] for i in range(6)] + pick(table, row_onehot(here, count), here)
+        records = arrived[:, part]
+        turned = jeffery([records[3 + i : 4 + i] for i in range(3)], rows)
+        out[0:3, part] = records[0:3]
+        for i in range(3):
+            out[3 + i : 4 + i, part] = turned[i]
+
+    turn(0)
+    bring.wait()
+    store.start()
+
+    @pl.loop(1, SLOT_DEV // width)
     def _(n):
-        base = pl.multiple_of(n * width, width)
-        here = cell[:, pl.ds(base, width)]
-        row = here // 128
-        row = (row % RCAP) * count + row // RCAP
-        onehot = (iota((256, width), 0) == row).astype(F32).astype(BF16)
-        picked = jnp.dot(table[...], jnp.concatenate([onehot, onehot], axis=0), preferred_element_type=F32)
-        lane = iota((128, width), 0) == here % 128
-        tensor = [
-            jnp.sum(jnp.where(lane, picked[128 * q : 128 * q + 128], 0.0), axis=0, keepdims=True) for q in range(9)
-        ]
-        records = arrived[:, pl.ds(base, width)]
-        turned = jeffery([records[3 + i : 4 + i] for i in range(3)], tensor)
-        out[0:3, pl.ds(base, width)] = records[0:3]
-        for i in range(3):
-            out[3 + i : 4 + i, pl.ds(base, width)] = turned[i]
-
-    copy.wait()
-
-
-def turn_call(recv, cell, arrived, flow):
+        turn(n)
+
+    store.wait()
+
+
+def turn_call(recv, tensor, cell, arrived, flow):
     return pl.pallas_call(
         turn_kernel,
         out_shape=(jax.ShapeDtypeStruct((6, SLOT_DEV), F32), jax.ShapeDtypeStruct(flow.shape, F32)),
-        in_specs=[vmem_spec()] * 3 + [any_spec()],
+        in_specs=[vmem_spec()] * 4 + [hbm_spec()],
         out_specs=(vmem_spec(), hbm_spec()),
-        scratch_shapes=[pltpu.VMEM((1152, 512), BF16), pltpu.SemaphoreType.DMA],
+        scratch_shapes=[
+            pltpu.VMEM((384, 2 * RCAP * recv.shape[0]), BF16),
+            pltpu.VMEM(flow.shape, F32),
+            pltpu.SemaphoreType.DMA,
+            pltpu.SemaphoreType.DMA,
+        ],
         compiler_params=pltpu.CompilerParams(vmem_limit_bytes=60 * MIB),
         name="gather_and_turn",
-    )(recv, cell, arrived, flow)
+    )(recv, tensor, cell, arrived, flow)
 
 
 def per_device(sizes, velocity, mean_flow, fibres, moves, grad_rows, grad_readers, fibre_cell):
-    flow, recv, arrived = flow_call(
+    cell = fibre_cell.reshape(1, SLOT_DEV)
+    flow, recv, tensor, arrived = flow_call(
         sizes, velocity, mean_flow.reshape(1, NY), fibres, moves.reshape(32, 128),
-        grad_rows.reshape(1, -1), grad_readers.reshape(1, -1),
+        grad_rows.reshape(1, -1), grad_readers.reshape(1, -1), cell,
     )
-    out, flow = turn_call(recv, fibre_cell.reshape(1, SLOT_DEV), arrived, flow)
+    out, flow = turn_call(recv, tensor, cell, arrived, flow)
     return flow, out
 
 

time: 147 us -> 57.1 us (0.39)
  Pallas kernels: 145 us -> 56.3 us
    pallas_call x1, Pallas kernels: 98.5 us -> 6.68 us  [turn_call(): pl.pallas_call(turn_kernel, out_shape=(jax.ShapeDtypeStruct((6, SLOT_DEV)...]
    pallas_call x1, Pallas kernels: 46.5 us -> 49.6 us  [flow_call(): pl.pallas_call(functools.partial(flow_kernel, sizes), out_shape=(jax.Shap...]
where the time goes in v3:
time: 57.1 us; the launch traced here: 57 us
  Pallas kernels  56.3 us (99%)
  between operations  0.64 us (1%)
    pallas_call x1, Pallas kernels, flow_call(): pl.pallas_call(functools.partial(flow_kernel, sizes), out_shape=(jax.Shap...  49.6 us
    pallas_call x1, Pallas kernels, turn_call(): pl.pallas_call(turn_kernel, out_shape=(jax.ShapeDtypeStruct((6, SLOT_DEV)...  6.68 us

profile of v3, /device:TPU:0, one launch (start us, length us, event | category | flops | bytes accessed | tf_op | source)
XLA Modules:
  0.0 57.0 jit_solution(14404395714793821474)
XLA Ops:
  0.6 49.6 %flow_and_rows.1 = (f32[3,16,64,256]{3,2,1,0:T(8,128)}, f32[128,8,128]{2,1,0:T(8,128)}, f32[6,5120]{1,0:T(8,128)}, f32[6,5120]{1,0:T(8,128)}) custom-call(f32[3,16,64,256]{3,2,1,0:T(8,128)} %velocity.1, f32[1,256]{1,0:T(1,128)} %bitcast.8, f32[6,4096]{1,0:T(8,128)} %fibres_hbm.1, s32[32,128]{1,0:T(8,128)} %bitcast.7, s32[1,192]{1,0:T(1,128)} %bitcast.9, ...), custom_call_target="tpu_custom_call" | custom-call | tf_op jit(solution)/shard_map/flow_and_rows/pallas_call | solution.py:378
  50.3 6.7 %gather_and_turn.1 = (f32[6,5120]{1,0:T(8,128)}, f32[3,16,64,256]{3,2,1,0:T(8,128)}) custom-call(f32[128,8,128]{2,1,0:T(8,128)} %get-tuple-element.8.recv, f32[6,5120]{1,0:T(8,128)} %get-tuple-element.9.tensor, s32[1,5120]{1,0:T(1,128)} %bitcast.6, f32[6,5120]{1,0:T(8,128)} %get-tuple-element.10.arrived, f32[3,16,64,256]{3,2,1,0:T(8,128)} %get-tuple-element.11.flow), custom_call_target="tpu_custom_call" | custom-call | tf_op jit(solution)/shard_map/gather_and_turn/pallas_call | solution.py:464

commit v4 on v3

--- a/solution.py
+++ b/solution.py
@@ -102,23 +102,24 @@
     rank, stay = fibre_ranks(code)
     fibre = iota((32, 128), 0) * 128 + iota((32, 128), 1)
     shift = as_row(jnp.where(code == 4, fibre - rank, 0))
-    slot = as_row(jnp.where(code == 4, -1, jnp.where(code < 4, code, code - 1) * CAP + rank))
+    group = as_row(jnp.where(code == 4, -1, jnp.where(code < 4, code, code - 1)))
+    rank = as_row(rank)
     split_ref[...] = jnp.zeros(split_ref.shape, F32)
     for i, part in enumerate(split3(fibres_ref[...])):
         split_ref[8 * i : 8 * i + 6, :] = part
-    acc = jnp.zeros((24, 8 * CAP), F32)
-    step = 512
+    acc = jnp.zeros((8 * 24, CAP), F32)
+    step = 1024
     for k in range(FIB_DEV // step):
-        onehot = (iota((8 * CAP, step), 0) == slot[:, k * step : k * step + step]).astype(F32).astype(BF16)
+        part = slice(k * step, k * step + step)
+        values = split_ref[:, part]
+        mine = jnp.concatenate([jnp.where(group[:, part] == j, values, 0.0) for j in range(8)], axis=0)
+        onehot = (iota((CAP, step), 0) == rank[:, part]).astype(F32).astype(BF16)
         acc = acc + lax.dot_general(
-            split_ref[:, k * step : k * step + step].astype(BF16),
-            onehot,
-            (((1,), (1,)), ((), ())),
-            preferred_element_type=F32,
+            mine.astype(BF16), onehot, (((1,), (1,)), ((), ())), preferred_element_type=F32
         )
-    packed = acc[0:6] + acc[8:14] + acc[16:22]
     for j in range(8):
-        pieces_ref[j] = packed[:, j * CAP : j * CAP + CAP]
+        own = acc[24 * j : 24 * j + 24]
+        pieces_ref[j] = own[0:6] + own[8:14] + own[16:22]
     records = fibres_ref[...]
     arrived_ref[:, 4 * CAP : 4 * CAP + FIB_DEV] = compact(records, jnp.broadcast_to(shift, records.shape), stay)
 
@@ -296,7 +297,7 @@
 
         @pl.loop(1, count)
         def _(i):
-            reader = lax.rem(me + i, count)
+            reader = lax.rem(me + i * (2 * lax.rem(me * 37, count // 2) + 1), count)
             pltpu.make_async_remote_copy(
                 send.at[c, reader, 0:6], recv.at[c, me, 0:6], row_send.at[c], row_recv.at[c],
                 device_id=place(reader, nz), device_id_type=MESH,
@@ -431,16 +432,29 @@
     return turned
 
 
-def turn_kernel(recv, tensor, cell, arrived, flow, out, flow_out, table, held, in_sem, out_sem):
-    bring = pltpu.make_async_copy(flow, held, in_sem)
-    bring.start()
-    store = pltpu.make_async_copy(held, flow_out, out_sem)
+def turn_kernel(
+    recv_hbm, tensor_hbm, cell_hbm, arrived_hbm, flow, out_hbm, flow_out,
+    recv, tensor, cell, arrived, out, table, held, in_sem, flow_in, flow_store, out_sem,
+):
+    loads = [
+        pltpu.make_async_copy(src, dst, in_sem.at[i])
+        for i, (src, dst) in enumerate(
+            ((recv_hbm, recv), (cell_hbm, cell), (tensor_hbm, tensor), (arrived_hbm, arrived))
+        )
+    ]
+    brings = [pltpu.make_async_copy(flow.at[c], held.at[c], flow_in.at[c]) for c in range(3)]
+    stores = [pltpu.make_async_copy(held.at[c], flow_out.at[c], flow_store.at[c]) for c in range(3)]
+    for copy in loads + brings:
+        copy.start()
     count = recv.shape[0]
+    loads[0].wait()
     fill_table(recv, table)
-    width = 1024
-
-    def turn(n):
-        part = pl.ds(pl.multiple_of(n * width, width), width)
+    for copy in loads[1:]:
+        copy.wait()
+    width = 1280
+    ends = []
+    for n in range(SLOT_DEV // width):
+        part = slice(n * width, n * width + width)
         here = cell[:, part]
         rows = [tensor[i : i + 1, part] for i in range(6)] + pick(table, row_onehot(here, count), here)
         records = arrived[:, part]
@@ -448,29 +462,31 @@
         out[0:3, part] = records[0:3]
         for i in range(3):
             out[3 + i : 4 + i, part] = turned[i]
-
-    turn(0)
-    bring.wait()
-    store.start()
-
-    @pl.loop(1, SLOT_DEV // width)
-    def _(n):
-        turn(n)
-
-    store.wait()
+        ends.append(pltpu.make_async_copy(out.at[:, part], out_hbm.at[:, part], out_sem.at[n]))
+        ends[-1].start()
+        if n < 3:
+            brings[n].wait()
+            stores[n].start()
+    for copy in stores + ends:
+        copy.wait()
 
 
 def turn_call(recv, tensor, cell, arrived, flow):
+    dma = pltpu.SemaphoreType.DMA
     return pl.pallas_call(
         turn_kernel,
         out_shape=(jax.ShapeDtypeStruct((6, SLOT_DEV), F32), jax.ShapeDtypeStruct(flow.shape, F32)),
-        in_specs=[vmem_spec()] * 4 + [hbm_spec()],
-        out_specs=(vmem_spec(), hbm_spec()),
+        in_specs=[hbm_spec()] * 5,
+        out_specs=(hbm_spec(), hbm_spec()),
         scratch_shapes=[
+            pltpu.VMEM(recv.shape, F32),
+            pltpu.VMEM(tensor.shape, F32),
+            pltpu.VMEM(cell.shape, I32),
+            pltpu.VMEM(arrived.shape, F32),
+            pltpu.VMEM((6, SLOT_DEV), F32),
             pltpu.VMEM((384, 2 * RCAP * recv.shape[0]), BF16),
             pltpu.VMEM(flow.shape, F32),
-            pltpu.SemaphoreType.DMA,
-            pltpu.SemaphoreType.DMA,
+            dma((4,)), dma((3,)), dma((3,)), dma((4,)),
         ],
         compiler_params=pltpu.CompilerParams(vmem_limit_bytes=60 * MIB),
         name="gather_and_turn",

time: 57.1 us -> 51.8 us (0.907)
  Pallas kernels: 56.3 us -> 50.8 us
    pallas_call x1, Pallas kernels: 49.6 us -> 44.6 us  [flow_call(): pl.pallas_call(functools.partial(flow_kernel, sizes), out_shape=(jax.Shap...]
where the time goes in v4:
time: 51.8 us; the launch traced here: 51.5 us
  Pallas kernels  50.8 us (98%)
  between operations  0.64 us (1%)
    pallas_call x1, Pallas kernels, flow_call(): pl.pallas_call(functools.partial(flow_kernel, sizes), out_shape=(jax.Shap...  44.6 us
    pallas_call x1, Pallas kernels, turn_call(): pl.pallas_call(turn_kernel, out_shape=(jax.ShapeDtypeStruct((6, SLOT_DEV)...  6.25 us

profile of v4, /device:TPU:0, one launch (start us, length us, event | category | flops | bytes accessed | tf_op | source)
XLA Modules:
  0.0 51.5 jit_solution(4855464823152315262)
XLA Ops:
  0.6 44.6 %flow_and_rows.1 = (f32[3,16,64,256]{3,2,1,0:T(8,128)}, f32[128,8,128]{2,1,0:T(8,128)}, f32[6,5120]{1,0:T(8,128)}, f32[6,5120]{1,0:T(8,128)}) custom-call(f32[3,16,64,256]{3,2,1,0:T(8,128)} %velocity.1, f32[1,256]{1,0:T(1,128)} %bitcast.8, f32[6,4096]{1,0:T(8,128)} %fibres_hbm.1, s32[32,128]{1,0:T(8,128)} %bitcast.7, s32[1,192]{1,0:T(1,128)} %bitcast.9, ...), custom_call_target="tpu_custom_call" | custom-call | tf_op jit(solution)/shard_map/flow_and_rows/pallas_call | solution.py:379
  45.2 6.3 %gather_and_turn.1 = (f32[6,5120]{1,0:T(8,128)}, f32[3,16,64,256]{3,2,1,0:T(8,128)}) custom-call(f32[128,8,128]{2,1,0:T(8,128)} %get-tuple-element.8.recv_hbm, f32[6,5120]{1,0:T(8,128)} %get-tuple-element.9.tensor_hbm, s32[1,5120]{1,0:T(1,128)} %bitcast.6, f32[6,5120]{1,0:T(8,128)} %get-tuple-element.10.arrived_hbm, f32[3,16,64,256]{3,2,1,0:T(8,128)} %get-tuple-element.11.flow), custom_call_target="tpu_custom_call" | custom-call | tf_op jit(solution)/shard_map/gather_and_turn/pallas_call | solution.py:476
